TPU v7x, 256 devices: a whole 4x4x8 slice. The times are simulated.
256 devices in a mesh: replica: 16 (over y_lo, x, core), fsdp: 16 (over z, y_hi).
Axes of the slice: x: 4, y: 4 (y_hi: 2, y_lo: 2; y = y_hi * 2 + y_lo), z: 8, core: 2. Of those that a mesh axis runs over, the one named last changes fastest.
Arguments:
- tokens: bfloat16 [65536, 8192], P(('replica', 'fsdp')), may hold values from -300 to 300
- norm_gain: float32 [16, 8192], P('replica'), may hold values from 0.5 to 1.5
- cotangent: bfloat16 [65536, 512], P(('replica', 'fsdp')), may hold values from -0.09375 to 0.09375
- value_weight: bfloat16 [16, 8192, 512], P('replica', 'fsdp'), may hold values from -0.03125 to 0.03125
- first_moment: float32 [16, 8192, 512], P('replica', 'fsdp'), may hold values from -3 to 3
- second_moment: float32 [16, 8192, 512], P('replica', 'fsdp'), may hold values from 0.1 to 2
- pseudo_grad: bfloat16 [16, 8192, 1024], P('replica', 'fsdp'), may hold values from -6 to 6
- fragment: float32 [8192, 1024], P(('fsdp', 'replica')), may hold values from -0.3 to 0.3
- outer_momentum: float32 [8192, 1024], P(('fsdp', 'replica')), may hold values from -3 to 3
Outputs:
- values: bfloat16 [65536, 512], P(('replica', 'fsdp'))
- new_value_weight: bfloat16 [16, 8192, 512], P('replica', 'fsdp')
- new_first: float32 [16, 8192, 512], P('replica', 'fsdp')
- new_second: float32 [16, 8192, 512], P('replica', 'fsdp')
- new_fragment: bfloat16 [8192, 1024], P('fsdp')
- new_outer_momentum: float32 [8192, 1024], P(('fsdp', 'replica'))
All inputs are finite; a program needn't handle non-finite values.
Results may differ from a plain program's by a relative error of at most 0.019.
Values may be sent and summed in bfloat16 or wider, within the bound.
No kernel may reach another device: no remote copies, remote signals or barrier semaphores. Data moves between devices by JAX's collectives and lax.ppermute only.
A program may use at most 128 MiB of HBM per device.

v0:
```python
import jax
import jax.numpy as jnp
from jax import lax
from jax.sharding import PartitionSpec as P


def contract_rows(left, right):
    return lax.dot_general(
        left, right, (((0,), (0,)), ((), ())), preferred_element_type=jnp.float32
    )


def body(
    tokens,
    norm_gain,
    cotangent,
    value_weight,
    first_moment,
    second_moment,
    pseudo_grad,
    fragment,
    outer_momentum,
):
    widened = tokens.astype(jnp.float32)
    inverse_rms = lax.rsqrt(jnp.mean(widened * widened, axis=-1, keepdims=True) + 1e-05)
    normed = (widened * inverse_rms * norm_gain).astype(jnp.bfloat16)
    weight = value_weight[0]
    columns = normed
    projected = jnp.dot(
        columns,
        lax.all_gather(weight, "fsdp", axis=0, tiled=True),
        preferred_element_type=jnp.float32,
    )
    columns = normed
    gradient = lax.psum_scatter(
        contract_rows(columns, cotangent), "fsdp", scatter_dimension=0, tiled=True
    )
    values = projected.astype(jnp.bfloat16)
    new_first = 0.9 * first_moment[0] + 0.1 * gradient
    new_second = 0.95 * second_moment[0] + 0.05 * gradient * gradient
    update = new_first / 0.6513215599 / (jnp.sqrt(new_second / 0.4012630607) + 1e-08)
    update = update + 0.1 * weight.astype(jnp.float32)
    new_weight = (weight.astype(jnp.float32) - 0.003 * update).astype(jnp.bfloat16)
    summed_grad = lax.psum_scatter(
        pseudo_grad[0], "replica", scatter_dimension=0, tiled=True
    ).astype(jnp.float32)
    average = summed_grad / lax.axis_size("replica")
    new_momentum = 0.9 * outer_momentum + average
    updated = (fragment - 0.7 * (average + 0.9 * new_momentum)).astype(jnp.bfloat16)
    new_fragment = lax.all_gather(updated, "replica", axis=0, tiled=True)
    return (values, new_weight[None], new_first[None], new_second[None], new_fragment, new_momentum)


def solution(mesh):
    return jax.shard_map(
        body,
        mesh=mesh,
        in_specs=(
            P(("replica", "fsdp"), None),
            P("replica", None),
            P(("replica", "fsdp"), None),
            P("replica", "fsdp", None),
            P("replica", "fsdp", None),
            P("replica", "fsdp", None),
            P("replica", "fsdp", None),
            P(("fsdp", "replica"), None),
            P(("fsdp", "replica"), None),
        ),
        out_specs=(
            P(("replica", "fsdp"), None),
            P("replica", "fsdp", None),
            P("replica", "fsdp", None),
            P("replica", "fsdp", None),
            P("fsdp", None),
            P(("fsdp", "replica"), None),
        ),
        check_vma=False,
    )
```

profile of v0, /device:TPU:2, one launch (start us, length us, event | category | flops | bytes accessed | tf_op | source)
XLA Modules:
  0.0 551.0 jit_solution(14806490370931666932)
XLA Ops:
  7.2 0.0 copy-start
  7.2 0.0 reduce-scatter.5.cloned.1.call-start
  7.2 0.7 reduce-scatter.5.cloned.1.call-update
  7.9 0.0 all-gather.4.cloned.1.call-start
  8.0 65.7 %reduce-scatter.5.cloned.1.call-done = bf16[32,1024]{1,0:T(8,128)(2,1)} async-done(((bf16[512,1024]{1,0:T(8,128)(2,1)}), bf16[32,1024]{1,0:T(8,128)(2,1)}) %reduce-scatter.5.cloned.1.call-update) | async-done | bytes 65552 | tf_op jit(solution)/shard_map/reduce_scatter | solution.py:44
  73.6 1.7 subtract_convert_fusion
  75.3 0.0 all-gather.4.cloned.1.call-update
  75.4 0.0 all-gather.6.cloned.1.call-start
  75.4 0.7 all-gather.6.cloned.1.call-update
  76.1 0.0 reduce-scatter.3.cloned.1.call-start
  76.1 3.1 fusion
  79.3 0.0 copy-done
  79.3 10.4 %fusion.8 = f32[8192,512]{1,0:T(8,128)} fusion(bf16[256,512]{1,0:T(8,128)(2,1)S(1)} %copy-done, bf16[256,8192]{1,0:T(8,128)(2,1)} %param.9, f32[8192]{0:T(1024)} %bitcast.32, f32[256]{0:T(256)S(1)} %add_rsqrt_fusion), kind=kOutput, calls=%fused_computation.11 | convolution fusion | flops 2155872256 | bytes 21267456 | tf_op jit(solution)/shard_map/dot_general | solution.py:8
  89.7 0.0 reduce-scatter.3.cloned.1.call-update
  89.7 0.0 copy-start.1
  89.7 0.0 copy-start.3
  89.8 23.6 %all-gather.4.cloned.1.call-done = bf16[512,1024]{1,0:T(8,128)(2,1)} async-done(((bf16[32,1024]{1,0:T(8,128)(2,1)}), bf16[512,1024]{1,0:T(8,128)(2,1)}) %all-gather.4.cloned.1.call-update) | async-done | bytes 1048592 | tf_op jit(solution)/shard_map/all_gather | solution.py:50
  113.3 139.2 %all-gather.6.cloned.1.call-done = bf16[1,8192,512]{2,1,0:T(8,128)(2,1)} async-done(((bf16[1,512,512]{2,1,0:T(8,128)(2,1)}), bf16[1,8192,512]{2,1,0:T(8,128)(2,1)}) %all-gather.6.cloned.1.call-update) | async-done | bytes 8388624 | tf_op jit(solution)/shard_map/all_gather | solution.py:31
  252.5 0.0 copy-done.4
  252.5 7.7 %fusion.5 = bf16[256,512]{1,0:T(8,128)(2,1)} fusion(bf16[1,8192,512]{2,1,0:T(8,128)(2,1)} %all-gather.6.cloned.1.call-done, bf16[256,8192]{1,0:T(8,128)(2,1)} %param.9, f32[8192]{0:T(1024)S(1)} %bitcast.33, f32[256]{0:T(256)S(1)} %add_rsqrt_fusion), kind=kOutput, calls=%fused_computation.10 | convolution fusion | flops 2156003328 | bytes 12878848 | tf_op jit(solution)/shard_map/dot_general | solution.py:29
  260.2 279.4 %reduce-scatter.3.cloned.1.call-done = f32[512,512]{1,0:T(8,128)} async-done(((f32[8192,512]{1,0:T(8,128)}), f32[512,512]{1,0:T(8,128)}) %reduce-scatter.3.cloned.1.call-update) | async-done | bytes 1048592 | tf_op jit(solution)/shard_map/reduce_scatter | solution.py:35
  539.6 0.0 copy-done.1
  539.6 3.9 fusion.17
  543.5 1.0 copy.16
  (5 shorter events, 0.0 us)
Async XLA Ops:
  7.2 72.1 %copy-start = (bf16[256,512]{1,0:T(8,128)(2,1)S(1)}, bf16[256,512]{1,0:T(8,128)(2,1)}, u32[]{:S(2)}) copy-start(bf16[256,512]{1,0:T(8,128)(2,1)} %param.11) | copy-start | bytes 786436
  7.2 66.4 %reduce-scatter.5.cloned.1.call-start = ((), (), s32[]{:S(2)}) async-start(), calls=%async_computation.3 | async-start | bytes 1114112 | tf_op jit(solution)/shard_map/reduce_scatter | solution.py:44
  7.9 105.4 %all-gather.4.cloned.1.call-start = ((), (), s32[]{:S(2)}) async-start(), calls=%async_computation.4 | async-start | bytes 1114112 | tf_op jit(solution)/shard_map/all_gather | solution.py:50
  75.4 177.1 %all-gather.6.cloned.1.call-start = ((), (), s32[]{:S(2)}) async-start(), calls=%async_computation.5 | async-start | bytes 8912896 | tf_op jit(solution)/shard_map/all_gather | solution.py:31
  76.1 463.5 %reduce-scatter.3.cloned.1.call-start = ((), (), s32[]{:S(2)}) async-start(), calls=%async_computation.2 | async-start | bytes 17825792 | tf_op jit(solution)/shard_map/reduce_scatter | solution.py:35
  89.7 162.8 %copy-start.4 = (f32[1,8192]{1,0:T(1,128)S(1)}, f32[1,8192]{1,0:T(1,128)}, u32[]{:S(2)}) copy-start(f32[1,8192]{1,0:T(1,128)} %param.10) | copy-start | bytes 98308
  89.7 449.9 %copy-start.1 = (bf16[1,512,512]{2,1,0:T(8,128)(2,1)S(1)}, bf16[1,512,512]{2,1,0:T(8,128)(2,1)}, u32[]{:S(2)}) copy-start(bf16[1,512,512]{2,1,0:T(8,128)(2,1)} %param.12) | copy-start | bytes 1572868
  89.7 449.9 %copy-start.3 = (f32[1,512,512]{2,1,0:T(8,128)S(1)}, f32[1,512,512]{2,1,0:T(8,128)}, u32[]{:S(2)}) copy-start(f32[1,512,512]{2,1,0:T(8,128)} %param.14) | copy-start | bytes 3145732
  113.3 430.2 %copy-start.2 = (bf16[512,1024]{1,0:T(8,128)(2,1)S(1)}, bf16[512,1024]{1,0:T(8,128)(2,1)}, u32[]{:S(2)}) copy-start(bf16[512,1024]{1,0:T(8,128)(2,1)} %all-gather.4.cloned.1.call-done) | copy-start | bytes 3145732
Sparse Core Ops, SparseCore 0:
  10.5 63.0 reduce-scatter.4
  76.2 37.0 all-gather.3
  116.2 136.1 all-gather.5
  257.0 282.5 reduce-scatter.2
where the time goes:
time: 551 us
  waiting for transfers between devices  509 us (92%)
  matrix products  18.2 us (3%)
  between operations  13.8 us (3%)
  other arithmetic  8.73 us (2%)
    reduce_scatter x1, waiting for transfers between devices, body(): lax.psum_scatter(contract_rows(columns, cotangent), 'fsdp', scatter_dimen...  279 us
    all_gather x1, waiting for transfers between devices, body(): lax.all_gather(weight, 'fsdp', axis=0, tiled=True)  139 us
    reduce_scatter x1, waiting for transfers between devices, body(): lax.psum_scatter(pseudo_grad[0], 'replica', scatter_dimension=0, tiled=True)  65.7 us
    all_gather x1, waiting for transfers between devices, body(): new_fragment = lax.all_gather(updated, 'replica', axis=0, tiled=True)  23.6 us
  transfers between devices with their start and end apart: 4, of which 4 were waited for; matrix products, arithmetic and copies ran while one was open for 4% of the time, Pallas kernels for 0%

commit v1 on v0

v1 whole, which is shorter than its diff:
```python
import jax
import jax.numpy as jnp
from jax import lax
from jax.experimental import pallas as pl
from jax.experimental.pallas import tpu as pltpu
from jax.sharding import Mesh, PartitionSpec as P

F32 = jnp.float32
BF16 = jnp.bfloat16
CORES, RING, COLUMN = 2, 8, 4
AROUND = [(z, (z + 1) % RING) for z in range(RING)] + [
    (RING + z, RING + (z - 1) % RING) for z in range(RING)
]
NEXT = [(0, 1), (1, 0), (2, 3), (3, 2)]
OUTER = [(0, 3), (3, 0), (1, 2), (2, 1)]
SWAP = [(0, 1), (1, 0)]
HINT = pl.CostEstimate(flops=4_000_000_000, bytes_accessed=20_000_000, transcendentals=0)
BRIEF = pl.CostEstimate(flops=1000, bytes_accessed=1000, transcendentals=0)


def around(value):
    return lax.ppermute(value, ("c", "z"), AROUND)


def matmul(left, right):
    return lax.dot_general(left, right, (((1,), (0,)), ((), ())), preferred_element_type=F32)


def contract_rows(left, right):
    return lax.dot_general(left, right, (((0,), (0,)), ((), ())), preferred_element_type=F32)


def whole(shape):
    return pl.BlockSpec(shape, lambda i, *_: (0,) * len(shape))


def lead(place, array):
    return pl.BlockSpec((1,) + array.shape[1:], lambda i, *_: (place,) + (0,) * (array.ndim - 1))


def tiled(shape, axis, tile):
    block = shape[:axis] + (tile,) + shape[axis + 1 :]
    return pl.BlockSpec(block, lambda i, *_: tuple(i if d == axis else 0 for d in range(len(shape))))


def turn(kernel, inputs, outs, scalars=None, steps=1, after=(), hint=HINT):
    arrays, specs = [a for a, _ in inputs], [s for _, s in inputs]
    for array in after:
        arrays.append(array)
        specs.append(whole((1,) * (array.ndim - 2) + (16, 128)))
    many = len(inputs)
    prefetched = [] if scalars is None else [jnp.stack([jnp.int32(s) for s in scalars])]

    def run(*refs):
        first = len(prefetched)
        ins, rest = refs[first : first + many], refs[first + len(arrays) :]
        kernel(refs[0] if prefetched else None, ins, rest)

    return pl.pallas_call(
        run,
        grid_spec=pltpu.PrefetchScalarGridSpec(
            num_scalar_prefetch=len(prefetched),
            grid=(steps,),
            in_specs=specs,
            out_specs=[s for _, s in outs],
        ),
        out_shape=[o for o, _ in outs],
        compiler_params=pltpu.CompilerParams(vmem_limit_bytes=16 * 2**20),
        cost_estimate=hint,
    )(*prefetched, *arrays)


def full(array):
    return array, whole(array.shape)


def new(shape, dtype):
    return jax.ShapeDtypeStruct(shape, dtype), whole(shape)


def far(array, blocks):
    return pltpu.with_memory_space_constraint(array, pltpu.HBM), blocks


def scaled(tokens_ref, gain_ref, inverse_rms, start, depth):
    at = pl.ds(pl.multiple_of(start, depth), depth)
    return (tokens_ref[:, at].astype(F32) * inverse_rms * gain_ref[:, at]).astype(BF16)


def first_block(start, tokens, norm_gain, depth):
    rows, width = tokens.shape
    tile = rows // 4

    def kernel(starts, ins, outs):
        tokens_ref, gain_ref = ins
        wide = tokens_ref[...].astype(F32)
        inverse_rms = lax.rsqrt(jnp.mean(wide * wide, axis=-1, keepdims=True) + 1e-05)
        outs[0][0] = scaled(tokens_ref, gain_ref, inverse_rms, starts[0], depth)
        outs[1][...] = jnp.broadcast_to(inverse_rms, outs[1].shape)

    block, inverse = (1, rows, depth), (rows, 128)
    return turn(
        kernel,
        [(tokens, tiled(tokens.shape, 0, tile)), full(norm_gain)],
        [
            (jax.ShapeDtypeStruct(block, BF16), tiled(block, 1, tile)),
            (jax.ShapeDtypeStruct(inverse, F32), tiled(inverse, 0, tile)),
        ],
        [start],
        4,
        hint=BRIEF,
    )


def normed_blocks(starts, sizes, tokens, norm_gain, inverse, depth, after=()):
    rows, width = tokens.shape
    tile = rows // 4

    def kernel(starts, ins, outs):
        tokens_ref, gain_ref, inverse_ref = ins
        at = 0
        for out, size in zip(outs, sizes):
            for place in range(size):
                out[place] = scaled(tokens_ref, gain_ref, inverse_ref[:, :1], starts[at], depth)
                at += 1

    shapes = [(size, rows, depth) for size in sizes]
    return turn(
        kernel,
        [
            (tokens, tiled(tokens.shape, 0, tile)),
            full(norm_gain),
            (inverse, tiled(inverse.shape, 0, tile)),
        ],
        [(pltpu.HBM(shape, BF16), tiled(shape, 1, tile)) for shape in shapes],
        starts,
        4,
        after,
    )


def copied(array, after):
    def kernel(_, ins, outs):
        outs[0][...] = ins[0][...]

    return turn(kernel, [full(array)], [new(array.shape, array.dtype)], after=after)[0]


def gradient_step(mine, theirs, cotangents, arrived, dtype, after=()):
    depth, columns = mine[0].shape[-1], cotangents[0].shape[1]
    inputs = [far(*mine), far(*theirs)] + [full(c) for c in cotangents]
    inputs += [] if arrived is None else [full(arrived)]

    def kernel(_, ins, outs):
        total = contract_rows(ins[0][0], ins[2][...]) + contract_rows(ins[1][0], ins[3][...])
        if arrived is not None:
            total = total + ins[4][...].astype(F32)
        outs[0][...] = total.astype(dtype)

    return turn(kernel, inputs, [new((depth, columns), dtype)], after=after)[0]


def value_step(mine, theirs, weights, sums, last=False, after=()):
    many = len(weights)
    rows, columns = mine[0][0].shape[1], weights[0].shape[1]
    inputs = [far(*m) for m in mine] + [far(*t) for t in theirs] + [full(w) for w in weights] + [full(s) for s in sums]

    def kernel(_, ins, outs):
        for side in range(2):
            value = sum(matmul(ins[side * many + p][0], ins[2 * many + p][...]) for p in range(many))
            if sums:
                value = value + ins[3 * many + side][...]
            outs[side][...] = value.astype(outs[side].dtype)

    shape = (rows, columns)
    return turn(kernel, inputs, [new(shape, F32), new(shape, BF16 if last else F32)], after=after)


def rows_of_core(parts, core, after):
    lines, columns, _, rows, width = parts.shape

    def kernel(_, ins, outs):
        outs[0][...] = ins[0][:, :, 0].swapaxes(0, 1)

    block = pl.BlockSpec((lines, columns, 1, rows, width), lambda i, core: (0, 0, core[0], 0, 0))
    return turn(kernel, [(parts, block)], [new((columns, lines, rows, width), BF16)], [core], 1, after, BRIEF)[0]


def sum_and_split(mine, got, picks, core=None, first=BF16, after=()):
    shape = got.shape
    sizes = [len(group) for group in picks]
    places = [p for group in picks for p in group]
    spec = whole(mine.shape)
    if core is not None:
        lines, columns, _, rows, width = mine.shape
        last = len(places)
        places.append(core)
        spec = pl.BlockSpec((lines, columns, 1, rows, width), lambda i, s: (0, 0, s[last], 0, 0))

    def kernel(places, ins, outs):
        at = 0
        for out, size in zip(outs, sizes):
            for place in range(size):
                index = places[at]
                held = ins[0][index] if core is None else ins[0][:, index, 0]
                out[place] = (held.astype(F32) + ins[1][index].astype(F32)).astype(out.dtype)
                at += 1

    outs = [new((size,) + shape[1:], first if out == 0 else BF16) for out, size in enumerate(sizes)]
    return turn(kernel, [(mine, spec), full(got)], outs, places, 1, after)


def outer_step(mine, got, fragment, momentum, after):
    def kernel(_, ins, outs):
        average = (ins[0][0] + ins[1][0].astype(F32)) / 16
        moved = 0.9 * ins[3][...] + average
        outs[0][0] = (ins[2][...] - 0.7 * (average + 0.9 * moved)).astype(BF16)
        outs[1][...] = moved

    shape = fragment.shape
    return turn(
        kernel,
        [full(mine), full(got), full(fragment), full(momentum)],
        [new((1,) + shape, BF16), new(shape, F32)],
        after=after,
    )


def join(mine, got, places, after=()):
    many = mine.shape[0]

    def kernel(places, ins, outs):
        for side in range(2):
            for place in range(many):
                outs[0][places[side * many + place]] = ins[side][place]

    return turn(kernel, [full(mine), full(got)], [new((2 * many,) + mine.shape[1:], BF16)], places, 1, after)[0]


def join_cores(core, mine, got):
    columns, lines, rows, width = mine.shape

    def kernel(core, ins, outs):
        for line in range(lines):
            for column in range(columns):
                outs[0][line, column, core[0]] = ins[0][column, line]
                outs[0][line, column, 1 - core[0]] = ins[1][column, line]

    return turn(kernel, [full(mine), full(got)], [new((lines, columns, CORES, rows, width), BF16)], [core])[0]


def body(
    tokens,
    norm_gain,
    cotangent,
    value_weight,
    first_moment,
    second_moment,
    pseudo_grad,
    fragment,
    outer_momentum,
):
    x, core, row = lax.axis_index("x"), lax.axis_index("c"), lax.axis_index("yl")
    z, half = lax.axis_index("z"), lax.axis_index("yh")
    way = 1 - 2 * core
    weight = value_weight[0]
    depth = weight.shape[0]
    parts = pseudo_grad[0].reshape(2, COLUMN, CORES, -1, pseudo_grad.shape[-1])

    blocks = [2 * ((z - (1 + step) * way) % RING) for step in range(RING)]
    gathered = [around(weight)]
    cotangents = (cotangent, lax.ppermute(cotangent, "yh", SWAP))
    sent, inverse = first_block((blocks[0] + 1 - half) * depth, tokens, norm_gain, depth)
    passed = copied(gathered[0], [sent])
    gathered.append(around(passed))

    starts = [(b + half) * depth for b in blocks] + [(b + 1 - half) * depth for b in blocks[1:]]
    before = [cotangents[1]]
    mine, *rest = normed_blocks(starts, (RING, 2, 3, 2), tokens, norm_gain, inverse, depth, before)
    theirs = []

    def send(sent):
        got = lax.ppermute(sent, "yh", SWAP)
        theirs.extend((got, lead(entry, got)) for entry in range(got.shape[0]))

    send(sent)
    send(rest[0])

    def products(steps, sums=(), last=False):
        return value_step(
            [(mine, lead(s, mine)) for s in steps],
            [theirs[s] for s in steps],
            [weight if s == RING - 1 else gathered[s] for s in steps],
            list(sums),
            last,
        )

    def outer_steps():
        after = yield
        got = lax.ppermute(given, "c", SWAP)
        beside = x ^ 1
        keep, give = sum_and_split(
            parts, got, ((x, 3 - x), (beside, 3 - beside)), core, BF16, [after]
        )
        got = lax.ppermute(give, "x", NEXT)
        after = yield give
        keep, give = sum_and_split(keep, got, ((0,), (1,)), None, BF16, [after])
        got = lax.ppermute(give, "x", OUTER)
        after = yield give
        keep, give = sum_and_split(keep[0], got[0], ((row,), (1 - row,)), None, F32, [after])
        got = lax.ppermute(give, "yl", SWAP)
        after = yield give
        held, new_momentum = outer_step(keep, got, fragment, outer_momentum, [after])
        got = lax.ppermute(held, "yl", SWAP)
        after = yield held
        held = join(held, got, (row, 1 - row), [after])
        got = lax.ppermute(held, "x", OUTER)
        after = yield held
        low = (x > 1).astype(jnp.int32)
        held = join(held[None], got[None], (low, 1 - low), [after])
        got = lax.ppermute(held, "x", NEXT)
        after = yield held
        ends = (x == 0) | (x == 3)
        first, second = jnp.where(ends, 0, 1), jnp.where(ends, 3, 2)
        held = join(held, got, (first, second, 1 - first, 5 - second), [after])
        got = lax.ppermute(held, "c", SWAP)
        yield held
        whole_fragment = join_cores(core, held, got)
        yield whole_fragment.reshape(-1, pseudo_grad.shape[-1]), new_momentum

    outer = outer_steps()
    next(outer)
    given = rows_of_core(parts, 1 - core, [sent])
    arrived, sums = None, ()
    for step in range(RING - 1):
        passed = gathered[step]
        if 0 < step < RING - 2:
            passed = copied(gathered[step], [total])
            gathered.append(around(passed))
        before = [passed, outer.send(mine if step == 0 else passed if step < RING - 2 else total)]
        if step in (2, 4):
            waiting = copied(rest[step // 2], [total])
            send(waiting)
            before.append(waiting)
        if step > 2:
            steps = ((0, 1), (2, 3), (4, 5), (6, 7))[step - 3]
            sums = products(steps, sums, step == RING - 2)
            before.append(sums[0])
        if step == RING - 2:
            own_gradient = gradient_step((mine, lead(RING - 1, mine)), theirs[-1], cotangents, None, F32)
            before.append(own_gradient)
        total = gradient_step(
            (mine, lead(step, mine)), theirs[step], cotangents, arrived, BF16, before
        )
        arrived = around(total)
    returned = lax.ppermute(sums[1], "yh", SWAP)
    values = (sums[0] + returned.astype(F32)).astype(BF16)
    new_fragment, new_momentum = outer.send(total)

    gradient = own_gradient + arrived.astype(F32)
    new_first = 0.9 * first_moment[0] + 0.1 * gradient
    new_second = 0.95 * second_moment[0] + 0.05 * gradient * gradient
    update = new_first / 0.6513215599 / (jnp.sqrt(new_second / 0.4012630607) + 1e-08)
    update = update + 0.1 * weight.astype(F32)
    new_weight = (weight.astype(F32) - 0.003 * update).astype(BF16)
    return (values, new_weight[None], new_first[None], new_second[None], new_fragment, new_momentum)


def solution(mesh):
    fine = Mesh(mesh.devices.reshape(2, COLUMN, CORES, RING, 2), ("yl", "x", "c", "z", "yh"))
    replica, fsdp = ("yl", "x", "c"), ("z", "yh")
    return jax.shard_map(
        body,
        mesh=fine,
        in_specs=(
            P(replica + fsdp, None),
            P(replica, None),
            P(replica + fsdp, None),
            P(replica, fsdp, None),
            P(replica, fsdp, None),
            P(replica, fsdp, None),
            P(replica, fsdp, None),
            P(fsdp + replica, None),
            P(fsdp + replica, None),
        ),
        out_specs=(
            P(replica + fsdp, None),
            P(replica, fsdp, None),
            P(replica, fsdp, None),
            P(replica, fsdp, None),
            P(fsdp, None),
            P(fsdp + replica, None),
        ),
        check_vma=False,
    )
```

time: 551 us -> 118 us (0.21)
  waiting for transfers between devices: 509 us -> 44.6 us
  Pallas kernels: 0 us -> 31.2 us
  starting transfers between devices: 0.16 us -> 28.6 us
  matrix products: 18.2 us -> 0 us
  between operations: 13.8 us -> 1.17 us
  local copies, waits for them, and re-layouts: 1 us -> 8.6 us
    reduce_scatter x2 -> x0, waiting for transfers between devices: 345 us -> none  [the longest x1 279 us: body(): lax.psum_scatter(contract_rows(columns, cotangent), 'fsdp', scatter_dimen...]
    all_gather x2 -> x0, waiting for transfers between devices: 163 us -> none  [the longest x1 139 us: body(): lax.all_gather(weight, 'fsdp', axis=0, tiled=True)]
    ppermute x0 -> x28, waiting for transfers between devices: none -> 44.6 us  [the longest x14 32.5 us: around(): return lax.ppermute(value, ('c', 'z'), AROUND)]
    pallas_call x0 -> x31, Pallas kernels: none -> 31.2 us  [turn(): pl.pallas_call(run, grid_spec=pltpu.PrefetchScalarGridSpec(num_scalar_pre...]
    ppermute x0 -> x28, starting transfers between devices: none -> 28.6 us  [the longest x4 7.52 us: send(): got = lax.ppermute(sent, 'yh', SWAP)]
    dot_general x2 -> x0, matrix products: 18.2 us -> none  [the longest x1 10.4 us: contract_rows(): lax.dot_general(left, right, (((0,), (0,)), ((), ())), preferred_element_...]
    unnamed x11 -> x38, local copies, waits for them, and re-layouts: 1 us -> 8.42 us
  transfers between devices with their start and end apart: 4 -> 28, of which waited for: 4 -> 14; matrix products, arithmetic and copies ran while one was open for 4% -> 1% of each run, Pallas kernels for 0% -> 26%
where the time goes in v1:
time: 118 us
  waiting for transfers between devices  44.6 us (38%)
  Pallas kernels  31.2 us (26%)
  starting transfers between devices  28.6 us (24%)
  local copies, waits for them, and re-layouts  8.6 us (7%)
  other arithmetic  3.45 us (3%)
    ppermute x14, waiting for transfers between devices, around(): return lax.ppermute(value, ('c', 'z'), AROUND)  32.5 us
    pallas_call x31, Pallas kernels, turn(): pl.pallas_call(run, grid_spec=pltpu.PrefetchScalarGridSpec(num_scalar_pre...  31.2 us
    unnamed x38, local copies, waits for them, and re-layouts  8.42 us
    ppermute x4, starting transfers between devices, send(): got = lax.ppermute(sent, 'yh', SWAP)  7.52 us
    ppermute x14, starting transfers between devices, around(): return lax.ppermute(value, ('c', 'z'), AROUND)  6.9 us
    ppermute x1, waiting for transfers between devices, outer_steps(): got = lax.ppermute(give, 'yl', SWAP)  5.53 us
    ppermute x4, waiting for transfers between devices, send(): got = lax.ppermute(sent, 'yh', SWAP)  3.34 us
    ppermute x1, starting transfers between devices, body(): cotangents = (cotangent, lax.ppermute(cotangent, 'yh', SWAP))  3.28 us
  transfers between devices with their start and end apart: 28, of which 14 were waited for; matrix products, arithmetic and copies ran while one was open for 1% of the time, Pallas kernels for 26%

profile of v1, /device:TPU:2, one launch (start us, length us, event | category | flops | bytes accessed | tf_op | source)
XLA Modules:
  0.0 117.6 jit_solution(17502983158592654073)
XLA Ops:
  0.6 3.3 %collective-permute-start = (bf16[256,512]{1,0:T(8,128)(2,1)}, bf16[256,512]{1,0:T(8,128)(2,1)}, u32[]{:S(2)}, u32[]{:S(2)}) collective-permute-start(bf16[256,512]{1,0:T(8,128)(2,1)} %refs_2_.21), channel_id=1, source_target_pairs={{0,1},{1,0},{2,3},{3,2},{4,5},{5,4},{6,7},{7,6},{8,9},{9,8},{10,11... | collective-permute-start | bytes 786440 | tf_op jit(solution)/shard_map/ppermute | solution.py:272
  3.9 2.2 %copy-done = bf16[256,8192]{1,0:T(8,128)(2,1)S(1)} copy-done((bf16[256,8192]{1,0:T(8,128)(2,1)S(1)}, bf16[256,8192]{1,0:T(8,128)(2,1)}, u32[]{:S(2)}) %copy-start) | copy-done | bytes 4194328
  9.3 2.0 %collective-permute-start.3 = (bf16[512,512]{1,0:T(8,128)(2,1)S(1)}, bf16[512,512]{1,0:T(8,128)(2,1)S(1)}, u32[]{:S(2)}, u32[]{:S(2)}) collective-permute-start(bf16[512,512]{1,0:T(8,128)(2,1)S(1)} %bitcast.58), channel_id=1, source_target_pairs={{0,2},{2,4},{4,6},{6,8},{8,10},{10,12},{12,14},{14,0},{16,30},{18,... | collective-permute-start | bytes 1572872 | tf_op jit(solution)/shard_map/ppermute | solution.py:22
  11.8 2.2 %copy-done.1 = bf16[256,8192]{1,0:T(8,128)(2,1)S(1)} copy-done((bf16[256,8192]{1,0:T(8,128)(2,1)S(1)}, bf16[256,8192]{1,0:T(8,128)(2,1)}, u32[]{:S(2)}) %copy-start.1) | copy-done | bytes 4194328
  14.9 4.0 %shard_map.137 = (bf16[8,256,512]{2,1,0:T(8,128)(2,1)}, bf16[2,256,512]{2,1,0:T(8,128)(2,1)}, bf16[3,256,512]{2,1,0:T(8,128)(2,1)}, bf16[2,256,512]{2,1,0:T(8,128)(2,1)}) custom-call(s32[15]{0:T(128)S(1)} %stack.124.refs_0_, bf16[256,8192]{1,0:T(8,128)(2,1)S(1)} %copy-done.1, f32[1,8192]{1,0:T(1,128)S(1)} %copy-done.5, f32[256,128]{1,0:T(8,128)S(1)} %copy-done.10, ...), custom_call_target="tpu_custom_call" | custom-call | flops 4000000000 | bytes 20000000 | tf_op jit(solution)/shard_map/pallas_call | solution.py:59
  18.9 3.2 %collective-permute-start.1 = (bf16[2,256,512]{2,1,0:T(8,128)(2,1)}, bf16[2,256,512]{2,1,0:T(8,128)(2,1)S(1)}, u32[]{:S(2)}, u32[]{:S(2)}) collective-permute-start(bf16[2,256,512]{2,1,0:T(8,128)(2,1)} %get-tuple-element.32), channel_id=1, source_target_pairs={{0,1},{1,0},{2,3},{3,2},{4,5},{5,4},{6,7},{7,6},{8,9},{9,8},{10,11... | collective-permute-start | bytes 1572872 | tf_op jit(solution)/shard_map/ppermute | solution.py:283
  27.1 2.0 %collective-permute-start.5 = (bf16[512,512]{1,0:T(8,128)(2,1)S(1)}, bf16[512,512]{1,0:T(8,128)(2,1)S(1)}, u32[]{:S(2)}, u32[]{:S(2)}) collective-permute-start(bf16[512,512]{1,0:T(8,128)(2,1)S(1)} %shard_map.140.refs_1_), channel_id=1, source_target_pairs={{0,2},{2,4},{4,6},{6,8},{8,10},{10,12},{12,14},{14,0},{16,30},{18,... | collective-permute-start | bytes 1572872 | tf_op jit(solution)/shard_map/ppermute | solution.py:22
  29.1 5.8 %collective-permute-done.6.refs_0_.refs_5_ = bf16[512,512]{1,0:T(8,128)(2,1)S(1)} collective-permute-done((bf16[512,512]{1,0:T(8,128)(2,1)S(1)}, bf16[512,512]{1,0:T(8,128)(2,1)S(1)}, u32[]{:S(2)}, u32[]{:S(2)}) %collective-permute-start.6) | collective-permute-done | bytes 524320 | tf_op jit(solution)/shard_map/ppermute | solution.py:22
  37.2 3.3 %collective-permute-done.5.refs_4_ = bf16[512,512]{1,0:T(8,128)(2,1)S(1)} collective-permute-done((bf16[512,512]{1,0:T(8,128)(2,1)S(1)}, bf16[512,512]{1,0:T(8,128)(2,1)S(1)}, u32[]{:S(2)}, u32[]{:S(2)}) %collective-permute-start.5) | collective-permute-done | bytes 524320 | tf_op jit(solution)/shard_map/ppermute | solution.py:22
  43.5 1.9 %shard_map.151 = (f32[256,512]{1,0:T(8,128)S(1)}, f32[256,512]{1,0:T(8,128)S(1)}) custom-call(bf16[8,256,512]{2,1,0:T(8,128)(2,1)} %get-tuple-element.29.refs_3_.refs_0_.refs_1_, bf16[8,256,512]{2,1,0:T(8,128)(2,1)} %get-tuple-element.29.refs_3_.refs_0_.refs_1_, bf16[1,256,512]{2,1,0:T(8,128)(2,1)} %collective-permute-done.2.refs_1_.refs_2_, ...), custom_call_target="tpu_custom_call" | custom-call | flops 4000000000 | bytes 20000000 | tf_op jit(solution)/shard_map/pallas_call | solution.py:59
  47.9 4.6 %collective-permute-done.9.refs_4_ = bf16[512,512]{1,0:T(8,128)(2,1)S(1)} collective-permute-done((bf16[512,512]{1,0:T(8,128)(2,1)S(1)}, bf16[512,512]{1,0:T(8,128)(2,1)S(1)}, u32[]{:S(2)}, u32[]{:S(2)}) %collective-permute-start.9) | collective-permute-done | bytes 524320 | tf_op jit(solution)/shard_map/ppermute | solution.py:22
  54.4 3.7 %collective-permute-done.13.refs_0_.refs_5_ = bf16[512,512]{1,0:T(8,128)(2,1)S(1)} collective-permute-done((bf16[512,512]{1,0:T(8,128)(2,1)S(1)}, bf16[512,512]{1,0:T(8,128)(2,1)S(1)}, u32[]{:S(2)}, u32[]{:S(2)}) %collective-permute-start.13) | collective-permute-done | bytes 524320 | tf_op jit(solution)/shard_map/ppermute | solution.py:22
  58.3 5.5 %collective-permute-done.14.refs_1_ = bf16[1,32,1024]{2,1,0:T(8,128)(2,1)S(1)} collective-permute-done((bf16[1,32,1024]{2,1,0:T(8,128)(2,1)S(1)}, bf16[1,32,1024]{2,1,0:T(8,128)(2,1)S(1)}, u32[]{:S(2)}, u32[]{:S(2)}) %collective-permute-start.14) | collective-permute-done | bytes 65568 | tf_op jit(solution)/shard_map/ppermute | solution.py:311
  68.6 2.7 %collective-permute-start.15 = (bf16[2,256,512]{2,1,0:T(8,128)(2,1)S(1)}, bf16[2,256,512]{2,1,0:T(8,128)(2,1)S(1)}, u32[]{:S(2)}, u32[]{:S(2)}) collective-permute-start(bf16[2,256,512]{2,1,0:T(8,128)(2,1)S(1)} %shard_map.153.refs_7_), channel_id=1, source_target_pairs={{0,1},{1,0},{2,3},{3,2},{4,5},{5,4},{6,7},{7,6},{8,9},{9,8},{10,11... | collective-permute-start | bytes 1572872 | tf_op jit(solution)/shard_map/ppermute | solution.py:283
  71.3 1.9 %shard_map.156 = (f32[256,512]{1,0:T(8,128)S(1)}, f32[256,512]{1,0:T(8,128)S(1)}) custom-call(bf16[8,256,512]{2,1,0:T(8,128)(2,1)} %get-tuple-element.29.refs_3_.refs_0_.refs_1_, bf16[8,256,512]{2,1,0:T(8,128)(2,1)} %get-tuple-element.29.refs_3_.refs_0_.refs_1_, bf16[2,256,512]{2,1,0:T(8,128)(2,1)} %copy-done.17, bf16[3,256,512]{2,1,0:T(8,128)(2,1)} %copy-done.16, ...), custom_call_target="tpu_custom_call" | custom-call | flops 4000000000 | bytes 20000000 | tf_op jit(solution)/shard_map/pallas_call | solution.py:59
  75.5 3.5 %collective-permute-done.18.refs_4_ = bf16[512,512]{1,0:T(8,128)(2,1)S(1)} collective-permute-done((bf16[512,512]{1,0:T(8,128)(2,1)S(1)}, bf16[512,512]{1,0:T(8,128)(2,1)S(1)}, u32[]{:S(2)}, u32[]{:S(2)}) %collective-permute-start.18) | collective-permute-done | bytes 524320 | tf_op jit(solution)/shard_map/ppermute | solution.py:22
  80.6 3.3 %collective-permute-done.15.refs_2_.refs_3_.refs_1_ = bf16[2,256,512]{2,1,0:T(8,128)(2,1)S(1)} collective-permute-done((bf16[2,256,512]{2,1,0:T(8,128)(2,1)S(1)}, bf16[2,256,512]{2,1,0:T(8,128)(2,1)S(1)}, u32[]{:S(2)}, u32[]{:S(2)}) %collective-permute-start.15) | collective-permute-done | bytes 524320 | tf_op jit(solution)/shard_map/ppermute | solution.py:283
  87.1 2.0 %collective-permute-start.25 = (bf16[2,2,32,1024]{3,2,1,0:T(8,128)(2,1)S(1)}, bf16[2,2,32,1024]{3,2,1,0:T(8,128)(2,1)S(1)}, u32[]{:S(2)}, u32[]{:S(2)}) collective-permute-start(bf16[2,2,32,1024]{3,2,1,0:T(8,128)(2,1)S(1)} %shard_map.162.refs_6_.refs_1_), channel_id=1, source_target_pairs={{0,32},{32,0},{64,96},{96,64},{1,33},{33,1},{65,97},{97,65},{2,34}... | collective-permute-start | bytes 786440 | tf_op jit(solution)/shard_map/ppermute | solution.py:321
  89.1 1.9 %shard_map.159 = (f32[256,512]{1,0:T(8,128)S(1)}, f32[256,512]{1,0:T(8,128)S(1)}) custom-call(bf16[8,256,512]{2,1,0:T(8,128)(2,1)} %get-tuple-element.29.refs_3_.refs_0_.refs_1_, bf16[8,256,512]{2,1,0:T(8,128)(2,1)} %get-tuple-element.29.refs_3_.refs_0_.refs_1_, bf16[3,256,512]{2,1,0:T(8,128)(2,1)} %copy-done.16, bf16[3,256,512]{2,1,0:T(8,128)(2,1)} %copy-done.16, ...), custom_call_target="tpu_custom_call" | custom-call | flops 4000000000 | bytes 20000000 | tf_op jit(solution)/shard_map/pallas_call | solution.py:59
  96.9 1.9 %shard_map.160 = (f32[256,512]{1,0:T(8,128)S(1)}, bf16[256,512]{1,0:T(8,128)(2,1)S(1)}) custom-call(bf16[8,256,512]{2,1,0:T(8,128)(2,1)} %get-tuple-element.29.refs_3_.refs_0_.refs_1_, bf16[8,256,512]{2,1,0:T(8,128)(2,1)} %get-tuple-element.29.refs_3_.refs_0_.refs_1_, bf16[2,256,512]{2,1,0:T(8,128)(2,1)} %copy-done.18, bf16[2,256,512]{2,1,0:T(8,128)(2,1)} %copy-done.18, ...), custom_call_target="tpu_custom_call" | custom-call | flops 4000000000 | bytes 20000000 | tf_op jit(solution)/shard_map/pallas_call | solution.py:59
  98.8 2.4 %collective-permute-start.21 = (bf16[256,512]{1,0:T(8,128)(2,1)S(1)}, bf16[256,512]{1,0:T(8,128)(2,1)S(1)}, u32[]{:S(2)}, u32[]{:S(2)}) collective-permute-start(bf16[256,512]{1,0:T(8,128)(2,1)S(1)} %get-tuple-element.48), channel_id=1, source_target_pairs={{0,1},{1,0},{2,3},{3,2},{4,5},{5,4},{6,7},{7,6},{8,9},{9,8},{10,11... | collective-permute-start | bytes 786440 | tf_op jit(solution)/shard_map/ppermute | solution.py:356
  101.2 1.9 %collective-permute-done.24.refs_4_ = bf16[512,512]{1,0:T(8,128)(2,1)S(1)} collective-permute-done((bf16[512,512]{1,0:T(8,128)(2,1)S(1)}, bf16[512,512]{1,0:T(8,128)(2,1)S(1)}, u32[]{:S(2)}, u32[]{:S(2)}) %collective-permute-start.24) | collective-permute-done | bytes 524320 | tf_op jit(solution)/shard_map/ppermute | solution.py:22
  108.1 7.1 %collective-permute-done.26 = bf16[512,512]{1,0:T(8,128)(2,1)S(1)} collective-permute-done((bf16[512,512]{1,0:T(8,128)(2,1)S(1)}, bf16[512,512]{1,0:T(8,128)(2,1)S(1)}, u32[]{:S(2)}, u32[]{:S(2)}) %collective-permute-start.26) | collective-permute-done | bytes 524320 | tf_op jit(solution)/shard_map/ppermute | solution.py:22
  115.1 2.4 %fusion.6 = (f32[1,512,512]{2,1,0:T(8,128)}, bf16[1,512,512]{2,1,0:T(8,128)(2,1)}, f32[1,512,512]{2,1,0:T(8,128)}) fusion(f32[512,512]{1,0:T(8,128)S(1)} %shard_map.161.refs_8_, bf16[512,512]{1,0:T(8,128)(2,1)S(1)} %collective-permute-done.26, f32[1,512,512]{2,1,0:T(8,128)S(1)} %copy-done.14, f32[1,512,512]{2,1,0:T(8,128)S(1)} %copy-done.15, ...), kind=kLoop, calls=%fused_computation.15 | loop fusion | flops 4980736 | bytes 6815744 | tf_op jit(solution)/shard_map/broadcast_in_dim | solution.py:366
  (109 shorter events, 41.8 us)
Async XLA Ops:
  0.6 11.1 %collective-permute-start = (bf16[256,512]{1,0:T(8,128)(2,1)}, bf16[256,512]{1,0:T(8,128)(2,1)}, u32[]{:S(2)}, u32[]{:S(2)}) collective-permute-start(bf16[256,512]{1,0:T(8,128)(2,1)} %refs_2_.21), channel_id=1, source_target_pairs={{0,1},{1,0},{2,3},{3,2},{4,5},{5,4},{6,7},{7,6},{8,9},{9,8},{10,11... | collective-permute-start | bytes 786440 | tf_op jit(solution)/shard_map/ppermute | solution.py:272
  8.8 16.7 %collective-permute-start.2 = (bf16[1,256,512]{2,1,0:T(8,128)(2,1)S(1)}, bf16[1,256,512]{2,1,0:T(8,128)(2,1)}, u32[]{:S(2)}, u32[]{:S(2)}) collective-permute-start(bf16[1,256,512]{2,1,0:T(8,128)(2,1)S(1)} %get-tuple-element.33.refs_2_.refs_1_), channel_id=1, source_target_pairs={{0,1},{1,0},{2,3},{3,2},{4,5},{5,4},{6,7},{7,6},{8,9},{9,8},{10,11... | collective-permute-start | bytes 786440 | tf_op jit(solution)/shard_map/ppermute | solution.py:283
  9.2 15.0 %collective-permute-start.4 = (bf16[4,2,32,1024]{3,2,1,0:T(8,128)(2,1)S(1)}, bf16[4,2,32,1024]{3,2,1,0:T(8,128)(2,1)S(1)}, u32[]{:S(2)}, u32[]{:S(2)}) collective-permute-start(bf16[4,2,32,1024]{3,2,1,0:T(8,128)(2,1)S(1)} %shard_map.138), channel_id=1, source_target_pairs={{0,16},{16,0},{1,17},{17,1},{2,18},{18,2},{3,19},{19,3},{4,20},{20... | collective-permute-start | bytes 1572872 | tf_op jit(solution)/shard_map/ppermute | solution.py:300
  9.3 13.1 %collective-permute-start.3 = (bf16[512,512]{1,0:T(8,128)(2,1)S(1)}, bf16[512,512]{1,0:T(8,128)(2,1)S(1)}, u32[]{:S(2)}, u32[]{:S(2)}) collective-permute-start(bf16[512,512]{1,0:T(8,128)(2,1)S(1)} %bitcast.58), channel_id=1, source_target_pairs={{0,2},{2,4},{4,6},{6,8},{8,10},{10,12},{12,14},{14,0},{16,30},{18,... | collective-permute-start | bytes 1572872 | tf_op jit(solution)/shard_map/ppermute | solution.py:22
  18.9 18.3 %collective-permute-start.1 = (bf16[2,256,512]{2,1,0:T(8,128)(2,1)}, bf16[2,256,512]{2,1,0:T(8,128)(2,1)S(1)}, u32[]{:S(2)}, u32[]{:S(2)}) collective-permute-start(bf16[2,256,512]{2,1,0:T(8,128)(2,1)} %get-tuple-element.32), channel_id=1, source_target_pairs={{0,1},{1,0},{2,3},{3,2},{4,5},{5,4},{6,7},{7,6},{8,9},{9,8},{10,11... | collective-permute-start | bytes 1572872 | tf_op jit(solution)/shard_map/ppermute | solution.py:283
  22.4 12.4 %collective-permute-start.6 = (bf16[512,512]{1,0:T(8,128)(2,1)S(1)}, bf16[512,512]{1,0:T(8,128)(2,1)S(1)}, u32[]{:S(2)}, u32[]{:S(2)}) collective-permute-start(bf16[512,512]{1,0:T(8,128)(2,1)S(1)} %shard_map.141), channel_id=1, source_target_pairs={{0,2},{2,4},{4,6},{6,8},{8,10},{10,12},{12,14},{14,0},{16,30},{18,... | collective-permute-start | bytes 1572872 | tf_op jit(solution)/shard_map/ppermute | solution.py:22
  24.9 10.1 %collective-permute-start.7 = (bf16[2,2,32,1024]{3,2,1,0:T(8,128)(2,1)S(1)}, bf16[2,2,32,1024]{3,2,1,0:T(8,128)(2,1)S(1)}, u32[]{:S(2)}, u32[]{:S(2)}) collective-permute-start(bf16[2,2,32,1024]{3,2,1,0:T(8,128)(2,1)S(1)} %get-tuple-element.34.refs_5_), channel_id=1, source_target_pairs={{0,32},{32,0},{64,96},{96,64},{1,33},{33,1},{65,97},{97,65},{2,34}... | collective-permute-start | bytes 786440 | tf_op jit(solution)/shard_map/ppermute | solution.py:305
  27.1 13.4 %collective-permute-start.5 = (bf16[512,512]{1,0:T(8,128)(2,1)S(1)}, bf16[512,512]{1,0:T(8,128)(2,1)S(1)}, u32[]{:S(2)}, u32[]{:S(2)}) collective-permute-start(bf16[512,512]{1,0:T(8,128)(2,1)S(1)} %shard_map.140.refs_1_), channel_id=1, source_target_pairs={{0,2},{2,4},{4,6},{6,8},{8,10},{10,12},{12,14},{14,0},{16,30},{18,... | collective-permute-start | bytes 1572872 | tf_op jit(solution)/shard_map/ppermute | solution.py:22
  34.9 11.2 %collective-permute-start.10 = (bf16[512,512]{1,0:T(8,128)(2,1)S(1)}, bf16[512,512]{1,0:T(8,128)(2,1)S(1)}, u32[]{:S(2)}, u32[]{:S(2)}) collective-permute-start(bf16[512,512]{1,0:T(8,128)(2,1)S(1)} %shard_map.142.refs_3_.refs_5_), channel_id=1, source_target_pairs={{0,2},{2,4},{4,6},{6,8},{8,10},{10,12},{12,14},{14,0},{16,30},{18,... | collective-permute-start | bytes 1572872 | tf_op jit(solution)/shard_map/ppermute | solution.py:22
  35.7 10.6 %collective-permute-start.11 = (bf16[1,2,32,1024]{3,2,1,0:T(8,128)(2,1)S(1)}, bf16[1,2,32,1024]{3,2,1,0:T(8,128)(2,1)S(1)}, u32[]{:S(2)}, u32[]{:S(2)}) collective-permute-start(bf16[1,2,32,1024]{3,2,1,0:T(8,128)(2,1)S(1)} %get-tuple-element.36.refs_6_), channel_id=1, source_target_pairs={{0,96},{96,0},{32,64},{64,32},{1,97},{97,1},{33,65},{65,33},{2,98}... | collective-permute-start | bytes 393224 | tf_op jit(solution)/shard_map/ppermute | solution.py:308
  42.1 10.5 %collective-permute-start.9 = (bf16[512,512]{1,0:T(8,128)(2,1)S(1)}, bf16[512,512]{1,0:T(8,128)(2,1)S(1)}, u32[]{:S(2)}, u32[]{:S(2)}) collective-permute-start(bf16[512,512]{1,0:T(8,128)(2,1)S(1)} %shard_map.144.refs_1_), channel_id=1, source_target_pairs={{0,2},{2,4},{4,6},{6,8},{8,10},{10,12},{12,14},{14,0},{16,30},{18,... | collective-permute-start | bytes 1572872 | tf_op jit(solution)/shard_map/ppermute | solution.py:22
  42.2 23.8 %collective-permute-start.8 = (bf16[3,256,512]{2,1,0:T(8,128)(2,1)S(1)}, bf16[3,256,512]{2,1,0:T(8,128)(2,1)S(1)}, u32[]{:S(2)}, u32[]{:S(2)}) collective-permute-start(bf16[3,256,512]{2,1,0:T(8,128)(2,1)S(1)} %shard_map.145.refs_7_), channel_id=1, source_target_pairs={{0,1},{1,0},{2,3},{3,2},{4,5},{5,4},{6,7},{7,6},{8,9},{9,8},{10,11... | collective-permute-start | bytes 2359304 | tf_op jit(solution)/shard_map/ppermute | solution.py:283
  46.1 12.0 %collective-permute-start.13 = (bf16[512,512]{1,0:T(8,128)(2,1)S(1)}, bf16[512,512]{1,0:T(8,128)(2,1)S(1)}, u32[]{:S(2)}, u32[]{:S(2)}) collective-permute-start(bf16[512,512]{1,0:T(8,128)(2,1)S(1)} %shard_map.146.refs_3_.refs_5_), channel_id=1, source_target_pairs={{0,2},{2,4},{4,6},{6,8},{8,10},{10,12},{12,14},{14,0},{16,30},{18,... | collective-permute-start | bytes 1572872 | tf_op jit(solution)/shard_map/ppermute | solution.py:22
  46.8 17.0 %collective-permute-start.14 = (bf16[1,32,1024]{2,1,0:T(8,128)(2,1)S(1)}, bf16[1,32,1024]{2,1,0:T(8,128)(2,1)S(1)}, u32[]{:S(2)}, u32[]{:S(2)}) collective-permute-start(bf16[1,32,1024]{2,1,0:T(8,128)(2,1)S(1)} %get-tuple-element.38.refs_6_), channel_id=1, source_target_pairs={{0,128},{128,0},{1,129},{129,1},{2,130},{130,2},{3,131},{131,3},{4... | collective-permute-start | bytes 196616 | tf_op jit(solution)/shard_map/ppermute | solution.py:311
  54.1 11.8 %collective-permute-start.12 = (bf16[512,512]{1,0:T(8,128)(2,1)S(1)}, bf16[512,512]{1,0:T(8,128)(2,1)S(1)}, u32[]{:S(2)}, u32[]{:S(2)}) collective-permute-start(bf16[512,512]{1,0:T(8,128)(2,1)S(1)} %shard_map.148.refs_1_), channel_id=1, source_target_pairs={{0,2},{2,4},{4,6},{6,8},{8,10},{10,12},{12,14},{14,0},{16,30},{18,... | collective-permute-start | bytes 1572872 | tf_op jit(solution)/shard_map/ppermute | solution.py:22
  58.2 15.0 %collective-permute-start.16 = (bf16[512,512]{1,0:T(8,128)(2,1)S(1)}, bf16[512,512]{1,0:T(8,128)(2,1)S(1)}, u32[]{:S(2)}, u32[]{:S(2)}) collective-permute-start(bf16[512,512]{1,0:T(8,128)(2,1)S(1)} %shard_map.149.refs_4_.refs_5_), channel_id=1, source_target_pairs={{0,2},{2,4},{4,6},{6,8},{8,10},{10,12},{12,14},{14,0},{16,30},{18,... | collective-permute-start | bytes 1572872 | tf_op jit(solution)/shard_map/ppermute | solution.py:22
  68.5 10.5 %collective-permute-start.18 = (bf16[512,512]{1,0:T(8,128)(2,1)S(1)}, bf16[512,512]{1,0:T(8,128)(2,1)S(1)}, u32[]{:S(2)}, u32[]{:S(2)}) collective-permute-start(bf16[512,512]{1,0:T(8,128)(2,1)S(1)} %shard_map.152.refs_1_), channel_id=1, source_target_pairs={{0,2},{2,4},{4,6},{6,8},{8,10},{10,12},{12,14},{14,0},{16,30},{18,... | collective-permute-start | bytes 1572872 | tf_op jit(solution)/shard_map/ppermute | solution.py:22
  68.6 15.3 %collective-permute-start.15 = (bf16[2,256,512]{2,1,0:T(8,128)(2,1)S(1)}, bf16[2,256,512]{2,1,0:T(8,128)(2,1)S(1)}, u32[]{:S(2)}, u32[]{:S(2)}) collective-permute-start(bf16[2,256,512]{2,1,0:T(8,128)(2,1)S(1)} %shard_map.153.refs_7_), channel_id=1, source_target_pairs={{0,1},{1,0},{2,3},{3,2},{4,5},{5,4},{6,7},{7,6},{8,9},{9,8},{10,11... | collective-permute-start | bytes 1572872 | tf_op jit(solution)/shard_map/ppermute | solution.py:283
  73.3 13.1 %collective-permute-start.17 = (bf16[512,512]{1,0:T(8,128)(2,1)S(1)}, bf16[512,512]{1,0:T(8,128)(2,1)S(1)}, u32[]{:S(2)}, u32[]{:S(2)}) collective-permute-start(bf16[512,512]{1,0:T(8,128)(2,1)S(1)} %shard_map.154.refs_3_.refs_5_), channel_id=1, source_target_pairs={{0,2},{2,4},{4,6},{6,8},{8,10},{10,12},{12,14},{14,0},{16,30},{18,... | collective-permute-start | bytes 1572872 | tf_op jit(solution)/shard_map/ppermute | solution.py:22
  74.0 12.5 %collective-permute-start.23 = (bf16[2,32,1024]{2,1,0:T(8,128)(2,1)S(1)}, bf16[2,32,1024]{2,1,0:T(8,128)(2,1)S(1)}, u32[]{:S(2)}, u32[]{:S(2)}) collective-permute-start(bf16[2,32,1024]{2,1,0:T(8,128)(2,1)S(1)} %shard_map.155.refs_6_), channel_id=1, source_target_pairs={{0,96},{96,0},{32,64},{64,32},{1,97},{97,1},{33,65},{65,33},{2,98}... | collective-permute-start | bytes 393224 | tf_op jit(solution)/shard_map/ppermute | solution.py:317
  80.5 10.5 %collective-permute-start.22 = (bf16[512,512]{1,0:T(8,128)(2,1)S(1)}, bf16[512,512]{1,0:T(8,128)(2,1)S(1)}, u32[]{:S(2)}, u32[]{:S(2)}) collective-permute-start(bf16[512,512]{1,0:T(8,128)(2,1)S(1)} %shard_map.157.refs_1_), channel_id=1, source_target_pairs={{0,2},{2,4},{4,6},{6,8},{8,10},{10,12},{12,14},{14,0},{16,30},{18,... | collective-permute-start | bytes 1572872 | tf_op jit(solution)/shard_map/ppermute | solution.py:22
  86.4 10.5 %collective-permute-start.20 = (bf16[512,512]{1,0:T(8,128)(2,1)S(1)}, bf16[512,512]{1,0:T(8,128)(2,1)S(1)}, u32[]{:S(2)}, u32[]{:S(2)}) collective-permute-start(bf16[512,512]{1,0:T(8,128)(2,1)S(1)} %shard_map.158.refs_3_.refs_5_), channel_id=1, source_target_pairs={{0,2},{2,4},{4,6},{6,8},{8,10},{10,12},{12,14},{14,0},{16,30},{18,... | collective-permute-start | bytes 1572872 | tf_op jit(solution)/shard_map/ppermute | solution.py:22
  92.6 10.5 %collective-permute-start.24 = (bf16[512,512]{1,0:T(8,128)(2,1)S(1)}, bf16[512,512]{1,0:T(8,128)(2,1)S(1)}, u32[]{:S(2)}, u32[]{:S(2)}) collective-permute-start(bf16[512,512]{1,0:T(8,128)(2,1)S(1)} %shard_map.163.refs_3_), channel_id=1, source_target_pairs={{0,2},{2,4},{4,6},{6,8},{8,10},{10,12},{12,14},{14,0},{16,30},{18,... | collective-permute-start | bytes 1572872 | tf_op jit(solution)/shard_map/ppermute | solution.py:22
  104.7 10.5 %collective-permute-start.26 = (bf16[512,512]{1,0:T(8,128)(2,1)S(1)}, bf16[512,512]{1,0:T(8,128)(2,1)S(1)}, u32[]{:S(2)}, u32[]{:S(2)}) collective-permute-start(bf16[512,512]{1,0:T(8,128)(2,1)S(1)} %shard_map.165), channel_id=1, source_target_pairs={{0,2},{2,4},{4,6},{6,8},{8,10},{10,12},{12,14},{14,0},{16,30},{18,... | collective-permute-start | bytes 1572872 | tf_op jit(solution)/shard_map/ppermute | solution.py:22
  (23 other events, 117.3 us)

commit v2 on v1

--- a/solution.py
+++ b/solution.py
@@ -14,7 +14,7 @@
 NEXT = [(0, 1), (1, 0), (2, 3), (3, 2)]
 OUTER = [(0, 3), (3, 0), (1, 2), (2, 1)]
 SWAP = [(0, 1), (1, 0)]
-HINT = pl.CostEstimate(flops=4_000_000_000, bytes_accessed=20_000_000, transcendentals=0)
+HINT = pl.CostEstimate(flops=2_500_000_000, bytes_accessed=12_000_000, transcendentals=0)
 BRIEF = pl.CostEstimate(flops=1000, bytes_accessed=1000, transcendentals=0)
 
 

time: 118 us -> 115 us (0.975)
  local copies, waits for them, and re-layouts: 8.6 us -> 7.03 us
  Pallas kernels: 31.2 us -> 29.9 us
    ppermute x4, waiting for transfers between devices: 3.34 us -> 0.04 us  [send(): got = lax.ppermute(sent, 'yh', SWAP)]
    ppermute x14, waiting for transfers between devices: 32.5 us -> 35.5 us  [around(): return lax.ppermute(value, ('c', 'z'), AROUND)]
    ppermute x1, starting transfers between devices: 0.09 us -> 3.02 us  [outer_steps(): got = lax.ppermute(given, 'c', SWAP)]
    ppermute x1, waiting for transfers between devices: 1.5 us -> 3.82 us  [body(): returned = lax.ppermute(sums[1], 'yh', SWAP)]
    ppermute x1, waiting for transfers between devices: 1.73 us -> 0.01 us  [outer_steps(): got = lax.ppermute(held, 'x', NEXT)]
    unnamed x38 -> x34, local copies, waits for them, and re-layouts: 8.42 us -> 6.85 us
    ppermute x1, starting transfers between devices: 2.01 us -> 0.62 us  [outer_steps(): got = lax.ppermute(held, 'x', NEXT)]
    pallas_call x31, Pallas kernels: 31.2 us -> 29.9 us  [turn(): pl.pallas_call(run, grid_spec=pltpu.PrefetchScalarGridSpec(num_scalar_pre...]
  transfers between devices with their start and end apart: 28 -> 28, of which waited for: 14 -> 13; matrix products, arithmetic and copies ran while one was open for 1% -> 1% of each run, Pallas kernels for 26% -> 26%
where the time goes in v2:
time: 115 us
  waiting for transfers between devices  44.7 us (39%)
  Pallas kernels  29.9 us (26%)
  starting transfers between devices  28.8 us (25%)
  local copies, waits for them, and re-layouts  7.03 us (6%)
  other arithmetic  3.44 us (3%)
    ppermute x14, waiting for transfers between devices, around(): return lax.ppermute(value, ('c', 'z'), AROUND)  35.5 us
    pallas_call x31, Pallas kernels, turn(): pl.pallas_call(run, grid_spec=pltpu.PrefetchScalarGridSpec(num_scalar_pre...  29.9 us
    ppermute x14, starting transfers between devices, around(): return lax.ppermute(value, ('c', 'z'), AROUND)  6.93 us
    unnamed x34, local copies, waits for them, and re-layouts  6.85 us
    ppermute x4, starting transfers between devices, send(): got = lax.ppermute(sent, 'yh', SWAP)  6.3 us
    ppermute x1, waiting for transfers between devices, outer_steps(): got = lax.ppermute(give, 'yl', SWAP)  5.36 us
    ppermute x1, waiting for transfers between devices, body(): returned = lax.ppermute(sums[1], 'yh', SWAP)  3.82 us
    ppermute x1, starting transfers between devices, body(): cotangents = (cotangent, lax.ppermute(cotangent, 'yh', SWAP))  3.19 us
  transfers between devices with their start and end apart: 28, of which 13 were waited for; matrix products, arithmetic and copies ran while one was open for 1% of the time, Pallas kernels for 26%

profile of v2, /device:TPU:2, one launch (start us, length us, event | category | flops | bytes accessed | tf_op | source)
XLA Modules:
  0.0 114.9 jit_solution(5892011931880525562)
XLA Ops:
  0.6 2.0 %collective-permute-start.3 = (bf16[512,512]{1,0:T(8,128)(2,1)}, bf16[512,512]{1,0:T(8,128)(2,1)S(1)}, u32[]{:S(2)}, u32[]{:S(2)}) collective-permute-start(bf16[512,512]{1,0:T(8,128)(2,1)} %bitcast.58), channel_id=1, source_target_pairs={{0,2},{2,4},{4,6},{6,8},{8,10},{10,12},{12,14},{14,0},{16,30},{18,... | collective-permute-start | bytes 1572872 | tf_op jit(solution)/shard_map/ppermute | solution.py:22
  2.6 3.2 %collective-permute-start = (bf16[256,512]{1,0:T(8,128)(2,1)}, bf16[256,512]{1,0:T(8,128)(2,1)S(1)}, u32[]{:S(2)}, u32[]{:S(2)}) collective-permute-start(bf16[256,512]{1,0:T(8,128)(2,1)} %refs_2_.21), channel_id=1, source_target_pairs={{0,1},{1,0},{2,3},{3,2},{4,5},{5,4},{6,7},{7,6},{8,9},{9,8},{10,11... | collective-permute-start | bytes 786440 | tf_op jit(solution)/shard_map/ppermute | solution.py:272
  5.8 2.2 %copy-done = bf16[256,8192]{1,0:T(8,128)(2,1)S(1)} copy-done((bf16[256,8192]{1,0:T(8,128)(2,1)S(1)}, bf16[256,8192]{1,0:T(8,128)(2,1)}, u32[]{:S(2)}) %copy-start) | copy-done | bytes 4194328
  10.5 3.0 %collective-permute-start.4 = (bf16[4,2,32,1024]{3,2,1,0:T(8,128)(2,1)S(1)}, bf16[4,2,32,1024]{3,2,1,0:T(8,128)(2,1)S(1)}, u32[]{:S(2)}, u32[]{:S(2)}) collective-permute-start(bf16[4,2,32,1024]{3,2,1,0:T(8,128)(2,1)S(1)} %shard_map.138), channel_id=1, source_target_pairs={{0,16},{16,0},{1,17},{17,1},{2,18},{18,2},{3,19},{19,3},{4,20},{20... | collective-permute-start | bytes 1572872 | tf_op jit(solution)/shard_map/ppermute | solution.py:300
  14.0 2.2 %copy-done.1 = bf16[256,8192]{1,0:T(8,128)(2,1)S(1)} copy-done((bf16[256,8192]{1,0:T(8,128)(2,1)S(1)}, bf16[256,8192]{1,0:T(8,128)(2,1)}, u32[]{:S(2)}) %copy-start.1) | copy-done | bytes 4194328
  16.2 3.4 %shard_map.137 = (bf16[8,256,512]{2,1,0:T(8,128)(2,1)}, bf16[2,256,512]{2,1,0:T(8,128)(2,1)}, bf16[3,256,512]{2,1,0:T(8,128)(2,1)}, bf16[2,256,512]{2,1,0:T(8,128)(2,1)}) custom-call(s32[15]{0:T(128)S(1)} %stack.124.refs_0_, bf16[256,8192]{1,0:T(8,128)(2,1)S(1)} %copy-done.1, f32[1,8192]{1,0:T(1,128)S(1)} %copy-done.5, ...), custom_call_target="tpu_custom_call" | custom-call | flops 2500000000 | bytes 12000000 | tf_op jit(solution)/shard_map/pallas_call | solution.py:59
  19.5 3.2 %collective-permute-start.1 = (bf16[2,256,512]{2,1,0:T(8,128)(2,1)}, bf16[2,256,512]{2,1,0:T(8,128)(2,1)S(1)}, u32[]{:S(2)}, u32[]{:S(2)}) collective-permute-start(bf16[2,256,512]{2,1,0:T(8,128)(2,1)} %get-tuple-element.32), channel_id=1, source_target_pairs={{0,1},{1,0},{2,3},{3,2},{4,5},{5,4},{6,7},{7,6},{8,9},{9,8},{10,11... | collective-permute-start | bytes 1572872 | tf_op jit(solution)/shard_map/ppermute | solution.py:283
  26.0 2.0 %collective-permute-start.5 = (bf16[512,512]{1,0:T(8,128)(2,1)S(1)}, bf16[512,512]{1,0:T(8,128)(2,1)S(1)}, u32[]{:S(2)}, u32[]{:S(2)}) collective-permute-start(bf16[512,512]{1,0:T(8,128)(2,1)S(1)} %shard_map.140.refs_1_), channel_id=1, source_target_pairs={{0,2},{2,4},{4,6},{6,8},{8,10},{10,12},{12,14},{14,0},{16,30},{18,... | collective-permute-start | bytes 1572872 | tf_op jit(solution)/shard_map/ppermute | solution.py:22
  28.0 5.5 %collective-permute-done.6.refs_0_.refs_5_ = bf16[512,512]{1,0:T(8,128)(2,1)S(1)} collective-permute-done((bf16[512,512]{1,0:T(8,128)(2,1)S(1)}, bf16[512,512]{1,0:T(8,128)(2,1)S(1)}, u32[]{:S(2)}, u32[]{:S(2)}) %collective-permute-start.6) | collective-permute-done | bytes 524320 | tf_op jit(solution)/shard_map/ppermute | solution.py:22
  35.9 3.2 %collective-permute-done.5.refs_4_ = bf16[512,512]{1,0:T(8,128)(2,1)S(1)} collective-permute-done((bf16[512,512]{1,0:T(8,128)(2,1)S(1)}, bf16[512,512]{1,0:T(8,128)(2,1)S(1)}, u32[]{:S(2)}, u32[]{:S(2)}) %collective-permute-start.5) | collective-permute-done | bytes 524320 | tf_op jit(solution)/shard_map/ppermute | solution.py:22
  41.7 3.1 %collective-permute-done.10.refs_0_.refs_4_ = bf16[512,512]{1,0:T(8,128)(2,1)S(1)} collective-permute-done((bf16[512,512]{1,0:T(8,128)(2,1)S(1)}, bf16[512,512]{1,0:T(8,128)(2,1)S(1)}, u32[]{:S(2)}, u32[]{:S(2)}) %collective-permute-start.10) | collective-permute-done | bytes 524320 | tf_op jit(solution)/shard_map/ppermute | solution.py:22
  45.5 5.6 %collective-permute-done.9.refs_4_ = bf16[512,512]{1,0:T(8,128)(2,1)S(1)} collective-permute-done((bf16[512,512]{1,0:T(8,128)(2,1)S(1)}, bf16[512,512]{1,0:T(8,128)(2,1)S(1)}, u32[]{:S(2)}, u32[]{:S(2)}) %collective-permute-start.9) | collective-permute-done | bytes 524320 | tf_op jit(solution)/shard_map/ppermute | solution.py:22
  52.7 1.9 %shard_map.151 = (f32[256,512]{1,0:T(8,128)S(1)}, f32[256,512]{1,0:T(8,128)S(1)}) custom-call(bf16[8,256,512]{2,1,0:T(8,128)(2,1)} %get-tuple-element.29.refs_3_.refs_0_.refs_1_, bf16[8,256,512]{2,1,0:T(8,128)(2,1)} %get-tuple-element.29.refs_3_.refs_0_.refs_1_, bf16[1,256,512]{2,1,0:T(8,128)(2,1)} %collective-permute-done.2.refs_1_.refs_2_, ...), custom_call_target="tpu_custom_call" | custom-call | flops 2500000000 | bytes 12000000 | tf_op jit(solution)/shard_map/pallas_call | solution.py:59
  56.9 5.4 %collective-permute-done.14.refs_1_ = bf16[1,32,1024]{2,1,0:T(8,128)(2,1)S(1)} collective-permute-done((bf16[1,32,1024]{2,1,0:T(8,128)(2,1)S(1)}, bf16[1,32,1024]{2,1,0:T(8,128)(2,1)S(1)}, u32[]{:S(2)}, u32[]{:S(2)}) %collective-permute-start.14) | collective-permute-done | bytes 65568 | tf_op jit(solution)/shard_map/ppermute | solution.py:311
  69.6 1.9 %shard_map.156 = (f32[256,512]{1,0:T(8,128)S(1)}, f32[256,512]{1,0:T(8,128)S(1)}) custom-call(bf16[8,256,512]{2,1,0:T(8,128)(2,1)} %get-tuple-element.29.refs_3_.refs_0_.refs_1_, bf16[8,256,512]{2,1,0:T(8,128)(2,1)} %get-tuple-element.29.refs_3_.refs_0_.refs_1_, bf16[2,256,512]{2,1,0:T(8,128)(2,1)} %copy-done.15, bf16[3,256,512]{2,1,0:T(8,128)(2,1)} %copy-done.14, ...), custom_call_target="tpu_custom_call" | custom-call | flops 2500000000 | bytes 12000000 | tf_op jit(solution)/shard_map/pallas_call | solution.py:59
  73.6 3.0 %collective-permute-done.18.refs_4_ = bf16[512,512]{1,0:T(8,128)(2,1)S(1)} collective-permute-done((bf16[512,512]{1,0:T(8,128)(2,1)S(1)}, bf16[512,512]{1,0:T(8,128)(2,1)S(1)}, u32[]{:S(2)}, u32[]{:S(2)}) %collective-permute-start.18) | collective-permute-done | bytes 524320 | tf_op jit(solution)/shard_map/ppermute | solution.py:22
  78.3 3.9 %collective-permute-done.17.refs_0_.refs_5_ = bf16[512,512]{1,0:T(8,128)(2,1)S(1)} collective-permute-done((bf16[512,512]{1,0:T(8,128)(2,1)S(1)}, bf16[512,512]{1,0:T(8,128)(2,1)S(1)}, u32[]{:S(2)}, u32[]{:S(2)}) %collective-permute-start.17) | collective-permute-done | bytes 524320 | tf_op jit(solution)/shard_map/ppermute | solution.py:22
  83.7 1.9 %shard_map.159 = (f32[256,512]{1,0:T(8,128)S(1)}, f32[256,512]{1,0:T(8,128)S(1)}) custom-call(bf16[8,256,512]{2,1,0:T(8,128)(2,1)} %get-tuple-element.29.refs_3_.refs_0_.refs_1_, bf16[8,256,512]{2,1,0:T(8,128)(2,1)} %get-tuple-element.29.refs_3_.refs_0_.refs_1_, bf16[3,256,512]{2,1,0:T(8,128)(2,1)} %copy-done.14, bf16[3,256,512]{2,1,0:T(8,128)(2,1)} %copy-done.14, ...), custom_call_target="tpu_custom_call" | custom-call | flops 2500000000 | bytes 12000000 | tf_op jit(solution)/shard_map/pallas_call | solution.py:59
  85.6 3.0 %collective-permute-done.22.refs_4_ = bf16[512,512]{1,0:T(8,128)(2,1)S(1)} collective-permute-done((bf16[512,512]{1,0:T(8,128)(2,1)S(1)}, bf16[512,512]{1,0:T(8,128)(2,1)S(1)}, u32[]{:S(2)}, u32[]{:S(2)}) %collective-permute-start.22) | collective-permute-done | bytes 524320 | tf_op jit(solution)/shard_map/ppermute | solution.py:22
  94.2 1.9 %shard_map.160 = (f32[256,512]{1,0:T(8,128)S(1)}, bf16[256,512]{1,0:T(8,128)(2,1)S(1)}) custom-call(bf16[8,256,512]{2,1,0:T(8,128)(2,1)} %get-tuple-element.29.refs_3_.refs_0_.refs_1_, bf16[8,256,512]{2,1,0:T(8,128)(2,1)} %get-tuple-element.29.refs_3_.refs_0_.refs_1_, bf16[2,256,512]{2,1,0:T(8,128)(2,1)} %copy-done.16, bf16[2,256,512]{2,1,0:T(8,128)(2,1)} %copy-done.16, ...), custom_call_target="tpu_custom_call" | custom-call | flops 2500000000 | bytes 12000000 | tf_op jit(solution)/shard_map/pallas_call | solution.py:59
  96.1 4.4 %collective-permute-done.24.refs_4_ = bf16[512,512]{1,0:T(8,128)(2,1)S(1)} collective-permute-done((bf16[512,512]{1,0:T(8,128)(2,1)S(1)}, bf16[512,512]{1,0:T(8,128)(2,1)S(1)}, u32[]{:S(2)}, u32[]{:S(2)}) %collective-permute-start.24) | collective-permute-done | bytes 524320 | tf_op jit(solution)/shard_map/ppermute | solution.py:22
  102.1 3.1 %collective-permute-start.21 = (bf16[256,512]{1,0:T(8,128)(2,1)S(1)}, bf16[256,512]{1,0:T(8,128)(2,1)S(1)}, u32[]{:S(2)}, u32[]{:S(2)}) collective-permute-start(bf16[256,512]{1,0:T(8,128)(2,1)S(1)} %get-tuple-element.48), channel_id=1, source_target_pairs={{0,1},{1,0},{2,3},{3,2},{4,5},{5,4},{6,7},{7,6},{8,9},{9,8},{10,11... | collective-permute-start | bytes 786440 | tf_op jit(solution)/shard_map/ppermute | solution.py:356
  106.3 3.8 %collective-permute-done.21 = bf16[256,512]{1,0:T(8,128)(2,1)S(1)} collective-permute-done((bf16[256,512]{1,0:T(8,128)(2,1)S(1)}, bf16[256,512]{1,0:T(8,128)(2,1)S(1)}, u32[]{:S(2)}, u32[]{:S(2)}) %collective-permute-start.21) | collective-permute-done | bytes 262176 | tf_op jit(solution)/shard_map/ppermute | solution.py:356
  112.5 2.4 %fusion.6 = (f32[1,512,512]{2,1,0:T(8,128)}, bf16[1,512,512]{2,1,0:T(8,128)(2,1)}, f32[1,512,512]{2,1,0:T(8,128)}) fusion(f32[512,512]{1,0:T(8,128)S(1)} %shard_map.161.refs_8_, bf16[512,512]{1,0:T(8,128)(2,1)S(1)} %collective-permute-done.26, f32[1,512,512]{2,1,0:T(8,128)S(1)} %copy-done.12, f32[1,512,512]{2,1,0:T(8,128)S(1)} %copy-done.13, ...), kind=kLoop, calls=%fused_computation.15 | loop fusion | flops 4980736 | bytes 6815744 | tf_op jit(solution)/shard_map/broadcast_in_dim | solution.py:366
  (105 shorter events, 38.7 us)
Async XLA Ops:
  0.6 22.1 %collective-permute-start.3 = (bf16[512,512]{1,0:T(8,128)(2,1)}, bf16[512,512]{1,0:T(8,128)(2,1)S(1)}, u32[]{:S(2)}, u32[]{:S(2)}) collective-permute-start(bf16[512,512]{1,0:T(8,128)(2,1)} %bitcast.58), channel_id=1, source_target_pairs={{0,2},{2,4},{4,6},{6,8},{8,10},{10,12},{12,14},{14,0},{16,30},{18,... | collective-permute-start | bytes 1572872 | tf_op jit(solution)/shard_map/ppermute | solution.py:22
  2.6 11.3 %collective-permute-start = (bf16[256,512]{1,0:T(8,128)(2,1)}, bf16[256,512]{1,0:T(8,128)(2,1)S(1)}, u32[]{:S(2)}, u32[]{:S(2)}) collective-permute-start(bf16[256,512]{1,0:T(8,128)(2,1)} %refs_2_.21), channel_id=1, source_target_pairs={{0,1},{1,0},{2,3},{3,2},{4,5},{5,4},{6,7},{7,6},{8,9},{9,8},{10,11... | collective-permute-start | bytes 786440 | tf_op jit(solution)/shard_map/ppermute | solution.py:272
  10.0 14.4 %collective-permute-start.2 = (bf16[1,256,512]{2,1,0:T(8,128)(2,1)S(1)}, bf16[1,256,512]{2,1,0:T(8,128)(2,1)}, u32[]{:S(2)}, u32[]{:S(2)}) collective-permute-start(bf16[1,256,512]{2,1,0:T(8,128)(2,1)S(1)} %get-tuple-element.33.refs_2_.refs_1_), channel_id=1, source_target_pairs={{0,1},{1,0},{2,3},{3,2},{4,5},{5,4},{6,7},{7,6},{8,9},{9,8},{10,11... | collective-permute-start | bytes 786440 | tf_op jit(solution)/shard_map/ppermute | solution.py:283
  10.5 12.6 %collective-permute-start.4 = (bf16[4,2,32,1024]{3,2,1,0:T(8,128)(2,1)S(1)}, bf16[4,2,32,1024]{3,2,1,0:T(8,128)(2,1)S(1)}, u32[]{:S(2)}, u32[]{:S(2)}) collective-permute-start(bf16[4,2,32,1024]{3,2,1,0:T(8,128)(2,1)S(1)} %shard_map.138), channel_id=1, source_target_pairs={{0,16},{16,0},{1,17},{17,1},{2,18},{18,2},{3,19},{19,3},{4,20},{20... | collective-permute-start | bytes 1572872 | tf_op jit(solution)/shard_map/ppermute | solution.py:300
  19.5 16.4 %collective-permute-start.1 = (bf16[2,256,512]{2,1,0:T(8,128)(2,1)}, bf16[2,256,512]{2,1,0:T(8,128)(2,1)S(1)}, u32[]{:S(2)}, u32[]{:S(2)}) collective-permute-start(bf16[2,256,512]{2,1,0:T(8,128)(2,1)} %get-tuple-element.32), channel_id=1, source_target_pairs={{0,1},{1,0},{2,3},{3,2},{4,5},{5,4},{6,7},{7,6},{8,9},{9,8},{10,11... | collective-permute-start | bytes 1572872 | tf_op jit(solution)/shard_map/ppermute | solution.py:283
  22.8 10.8 %collective-permute-start.6 = (bf16[512,512]{1,0:T(8,128)(2,1)S(1)}, bf16[512,512]{1,0:T(8,128)(2,1)S(1)}, u32[]{:S(2)}, u32[]{:S(2)}) collective-permute-start(bf16[512,512]{1,0:T(8,128)(2,1)S(1)} %shard_map.141), channel_id=1, source_target_pairs={{0,2},{2,4},{4,6},{6,8},{8,10},{10,12},{12,14},{14,0},{16,30},{18,... | collective-permute-start | bytes 1572872 | tf_op jit(solution)/shard_map/ppermute | solution.py:22
  23.9 9.8 %collective-permute-start.7 = (bf16[2,2,32,1024]{3,2,1,0:T(8,128)(2,1)S(1)}, bf16[2,2,32,1024]{3,2,1,0:T(8,128)(2,1)S(1)}, u32[]{:S(2)}, u32[]{:S(2)}) collective-permute-start(bf16[2,2,32,1024]{3,2,1,0:T(8,128)(2,1)S(1)} %get-tuple-element.34.refs_5_), channel_id=1, source_target_pairs={{0,32},{32,0},{64,96},{96,64},{1,33},{33,1},{65,97},{97,65},{2,34}... | collective-permute-start | bytes 786440 | tf_op jit(solution)/shard_map/ppermute | solution.py:305
  26.0 13.2 %collective-permute-start.5 = (bf16[512,512]{1,0:T(8,128)(2,1)S(1)}, bf16[512,512]{1,0:T(8,128)(2,1)S(1)}, u32[]{:S(2)}, u32[]{:S(2)}) collective-permute-start(bf16[512,512]{1,0:T(8,128)(2,1)S(1)} %shard_map.140.refs_1_), channel_id=1, source_target_pairs={{0,2},{2,4},{4,6},{6,8},{8,10},{10,12},{12,14},{14,0},{16,30},{18,... | collective-permute-start | bytes 1572872 | tf_op jit(solution)/shard_map/ppermute | solution.py:22
  33.6 11.2 %collective-permute-start.10 = (bf16[512,512]{1,0:T(8,128)(2,1)S(1)}, bf16[512,512]{1,0:T(8,128)(2,1)S(1)}, u32[]{:S(2)}, u32[]{:S(2)}) collective-permute-start(bf16[512,512]{1,0:T(8,128)(2,1)S(1)} %shard_map.142.refs_3_.refs_5_), channel_id=1, source_target_pairs={{0,2},{2,4},{4,6},{6,8},{8,10},{10,12},{12,14},{14,0},{16,30},{18,... | collective-permute-start | bytes 1572872 | tf_op jit(solution)/shard_map/ppermute | solution.py:22
  34.3 10.6 %collective-permute-start.11 = (bf16[1,2,32,1024]{3,2,1,0:T(8,128)(2,1)S(1)}, bf16[1,2,32,1024]{3,2,1,0:T(8,128)(2,1)S(1)}, u32[]{:S(2)}, u32[]{:S(2)}) collective-permute-start(bf16[1,2,32,1024]{3,2,1,0:T(8,128)(2,1)S(1)} %get-tuple-element.36.refs_6_), channel_id=1, source_target_pairs={{0,96},{96,0},{32,64},{64,32},{1,97},{97,1},{33,65},{65,33},{2,98}... | collective-permute-start | bytes 393224 | tf_op jit(solution)/shard_map/ppermute | solution.py:308
  40.7 10.5 %collective-permute-start.9 = (bf16[512,512]{1,0:T(8,128)(2,1)S(1)}, bf16[512,512]{1,0:T(8,128)(2,1)S(1)}, u32[]{:S(2)}, u32[]{:S(2)}) collective-permute-start(bf16[512,512]{1,0:T(8,128)(2,1)S(1)} %shard_map.144.refs_1_), channel_id=1, source_target_pairs={{0,2},{2,4},{4,6},{6,8},{8,10},{10,12},{12,14},{14,0},{16,30},{18,... | collective-permute-start | bytes 1572872 | tf_op jit(solution)/shard_map/ppermute | solution.py:22
  40.8 22.9 %collective-permute-start.8 = (bf16[3,256,512]{2,1,0:T(8,128)(2,1)S(1)}, bf16[3,256,512]{2,1,0:T(8,128)(2,1)S(1)}, u32[]{:S(2)}, u32[]{:S(2)}) collective-permute-start(bf16[3,256,512]{2,1,0:T(8,128)(2,1)S(1)} %shard_map.145.refs_7_), channel_id=1, source_target_pairs={{0,1},{1,0},{2,3},{3,2},{4,5},{5,4},{6,7},{7,6},{8,9},{9,8},{10,11... | collective-permute-start | bytes 2359304 | tf_op jit(solution)/shard_map/ppermute | solution.py:283
  44.8 11.9 %collective-permute-start.13 = (bf16[512,512]{1,0:T(8,128)(2,1)S(1)}, bf16[512,512]{1,0:T(8,128)(2,1)S(1)}, u32[]{:S(2)}, u32[]{:S(2)}) collective-permute-start(bf16[512,512]{1,0:T(8,128)(2,1)S(1)} %shard_map.146.refs_3_.refs_5_), channel_id=1, source_target_pairs={{0,2},{2,4},{4,6},{6,8},{8,10},{10,12},{12,14},{14,0},{16,30},{18,... | collective-permute-start | bytes 1572872 | tf_op jit(solution)/shard_map/ppermute | solution.py:22
  52.6 11.1 %collective-permute-start.12 = (bf16[512,512]{1,0:T(8,128)(2,1)S(1)}, bf16[512,512]{1,0:T(8,128)(2,1)S(1)}, u32[]{:S(2)}, u32[]{:S(2)}) collective-permute-start(bf16[512,512]{1,0:T(8,128)(2,1)S(1)} %shard_map.148.refs_1_), channel_id=1, source_target_pairs={{0,2},{2,4},{4,6},{6,8},{8,10},{10,12},{12,14},{14,0},{16,30},{18,... | collective-permute-start | bytes 1572872 | tf_op jit(solution)/shard_map/ppermute | solution.py:22
  56.8 12.6 %collective-permute-start.16 = (bf16[512,512]{1,0:T(8,128)(2,1)S(1)}, bf16[512,512]{1,0:T(8,128)(2,1)S(1)}, u32[]{:S(2)}, u32[]{:S(2)}) collective-permute-start(bf16[512,512]{1,0:T(8,128)(2,1)S(1)} %shard_map.149.refs_4_.refs_5_), channel_id=1, source_target_pairs={{0,2},{2,4},{4,6},{6,8},{8,10},{10,12},{12,14},{14,0},{16,30},{18,... | collective-permute-start | bytes 1572872 | tf_op jit(solution)/shard_map/ppermute | solution.py:22
  66.1 10.5 %collective-permute-start.18 = (bf16[512,512]{1,0:T(8,128)(2,1)S(1)}, bf16[512,512]{1,0:T(8,128)(2,1)S(1)}, u32[]{:S(2)}, u32[]{:S(2)}) collective-permute-start(bf16[512,512]{1,0:T(8,128)(2,1)S(1)} %shard_map.152.refs_1_), channel_id=1, source_target_pairs={{0,2},{2,4},{4,6},{6,8},{8,10},{10,12},{12,14},{14,0},{16,30},{18,... | collective-permute-start | bytes 1572872 | tf_op jit(solution)/shard_map/ppermute | solution.py:22
  67.6 23.3 %collective-permute-start.15 = (bf16[2,256,512]{2,1,0:T(8,128)(2,1)S(1)}, bf16[2,256,512]{2,1,0:T(8,128)(2,1)S(1)}, u32[]{:S(2)}, u32[]{:S(2)}) collective-permute-start(bf16[2,256,512]{2,1,0:T(8,128)(2,1)S(1)} %shard_map.153.refs_7_), channel_id=1, source_target_pairs={{0,1},{1,0},{2,3},{3,2},{4,5},{5,4},{6,7},{7,6},{8,9},{9,8},{10,11... | collective-permute-start | bytes 1572872 | tf_op jit(solution)/shard_map/ppermute | solution.py:283
  69.4 12.8 %collective-permute-start.17 = (bf16[512,512]{1,0:T(8,128)(2,1)S(1)}, bf16[512,512]{1,0:T(8,128)(2,1)S(1)}, u32[]{:S(2)}, u32[]{:S(2)}) collective-permute-start(bf16[512,512]{1,0:T(8,128)(2,1)S(1)} %shard_map.154.refs_3_.refs_5_), channel_id=1, source_target_pairs={{0,2},{2,4},{4,6},{6,8},{8,10},{10,12},{12,14},{14,0},{16,30},{18,... | collective-permute-start | bytes 1572872 | tf_op jit(solution)/shard_map/ppermute | solution.py:22
  72.1 10.4 %collective-permute-start.23 = (bf16[2,32,1024]{2,1,0:T(8,128)(2,1)S(1)}, bf16[2,32,1024]{2,1,0:T(8,128)(2,1)S(1)}, u32[]{:S(2)}, u32[]{:S(2)}) collective-permute-start(bf16[2,32,1024]{2,1,0:T(8,128)(2,1)S(1)} %shard_map.155.refs_6_), channel_id=1, source_target_pairs={{0,96},{96,0},{32,64},{64,32},{1,97},{97,1},{33,65},{65,33},{2,98}... | collective-permute-start | bytes 393224 | tf_op jit(solution)/shard_map/ppermute | solution.py:317
  78.1 10.5 %collective-permute-start.22 = (bf16[512,512]{1,0:T(8,128)(2,1)S(1)}, bf16[512,512]{1,0:T(8,128)(2,1)S(1)}, u32[]{:S(2)}, u32[]{:S(2)}) collective-permute-start(bf16[512,512]{1,0:T(8,128)(2,1)S(1)} %shard_map.157.refs_1_), channel_id=1, source_target_pairs={{0,2},{2,4},{4,6},{6,8},{8,10},{10,12},{12,14},{14,0},{16,30},{18,... | collective-permute-start | bytes 1572872 | tf_op jit(solution)/shard_map/ppermute | solution.py:22
  82.3 11.9 %collective-permute-start.20 = (bf16[512,512]{1,0:T(8,128)(2,1)S(1)}, bf16[512,512]{1,0:T(8,128)(2,1)S(1)}, u32[]{:S(2)}, u32[]{:S(2)}) collective-permute-start(bf16[512,512]{1,0:T(8,128)(2,1)S(1)} %shard_map.158.refs_3_.refs_5_), channel_id=1, source_target_pairs={{0,2},{2,4},{4,6},{6,8},{8,10},{10,12},{12,14},{14,0},{16,30},{18,... | collective-permute-start | bytes 1572872 | tf_op jit(solution)/shard_map/ppermute | solution.py:22
  90.1 10.5 %collective-permute-start.24 = (bf16[512,512]{1,0:T(8,128)(2,1)S(1)}, bf16[512,512]{1,0:T(8,128)(2,1)S(1)}, u32[]{:S(2)}, u32[]{:S(2)}) collective-permute-start(bf16[512,512]{1,0:T(8,128)(2,1)S(1)} %shard_map.163.refs_3_), channel_id=1, source_target_pairs={{0,2},{2,4},{4,6},{6,8},{8,10},{10,12},{12,14},{14,0},{16,30},{18,... | collective-permute-start | bytes 1572872 | tf_op jit(solution)/shard_map/ppermute | solution.py:22
  90.8 14.5 %collective-permute-start.27 = (bf16[4,2,32,1024]{3,2,1,0:T(8,128)(2,1)S(1)}, bf16[4,2,32,1024]{3,2,1,0:T(8,128)(2,1)S(1)}, u32[]{:S(2)}, u32[]{:S(2)}) collective-permute-start(bf16[4,2,32,1024]{3,2,1,0:T(8,128)(2,1)S(1)} %shard_map.164.refs_6_.refs_1_), channel_id=1, source_target_pairs={{0,16},{16,0},{1,17},{17,1},{2,18},{18,2},{3,19},{19,3},{4,20},{20... | collective-permute-start | bytes 1572872 | tf_op jit(solution)/shard_map/ppermute | solution.py:326
  102.0 10.5 %collective-permute-start.26 = (bf16[512,512]{1,0:T(8,128)(2,1)S(1)}, bf16[512,512]{1,0:T(8,128)(2,1)S(1)}, u32[]{:S(2)}, u32[]{:S(2)}) collective-permute-start(bf16[512,512]{1,0:T(8,128)(2,1)S(1)} %shard_map.165), channel_id=1, source_target_pairs={{0,2},{2,4},{4,6},{6,8},{8,10},{10,12},{12,14},{14,0},{16,30},{18,... | collective-permute-start | bytes 1572872 | tf_op jit(solution)/shard_map/ppermute | solution.py:22
  (21 other events, 110.1 us)

commit v3 on v2

--- a/solution.py
+++ b/solution.py
@@ -331,13 +331,16 @@
     outer = outer_steps()
     next(outer)
     given = rows_of_core(parts, 1 - core, [sent])
-    arrived, sums = None, ()
+    arrived, sums, turns = None, (), []
     for step in range(RING - 1):
         passed = gathered[step]
         if 0 < step < RING - 2:
             passed = copied(gathered[step], [total])
             gathered.append(around(passed))
-        before = [passed, outer.send(mine if step == 0 else passed if step < RING - 2 else total)]
+        before = [passed]
+        turned = outer.send(mine if step == 0 else passed if step < RING - 2 else total)
+        turns.append(turned)
+        before += {2: turns[1:2], 3: turns[2:3], 4: turns[3:5], 5: turns[5:], 6: turns[6:]}.get(step, [])
         if step in (2, 4):
             waiting = copied(rest[step // 2], [total])
             send(waiting)

time: 115 us -> 115 us (level)
  no operation moved by 1% of the time
where the time goes in v3:
time: 115 us
  waiting for transfers between devices  44.7 us (39%)
  Pallas kernels  29.9 us (26%)
  starting transfers between devices  28.7 us (25%)
  local copies, waits for them, and re-layouts  7.03 us (6%)
  other arithmetic  3.44 us (3%)
    ppermute x14, waiting for transfers between devices, around(): return lax.ppermute(value, ('c', 'z'), AROUND)  35.5 us
    pallas_call x31, Pallas kernels, turn(): pl.pallas_call(run, grid_spec=pltpu.PrefetchScalarGridSpec(num_scalar_pre...  29.9 us
    ppermute x14, starting transfers between devices, around(): return lax.ppermute(value, ('c', 'z'), AROUND)  6.92 us
    unnamed x34, local copies, waits for them, and re-layouts  6.85 us
    ppermute x4, starting transfers between devices, send(): got = lax.ppermute(sent, 'yh', SWAP)  6.31 us
    ppermute x1, waiting for transfers between devices, outer_steps(): got = lax.ppermute(give, 'yl', SWAP)  5.36 us
    ppermute x1, waiting for transfers between devices, body(): returned = lax.ppermute(sums[1], 'yh', SWAP)  3.81 us
    ppermute x1, starting transfers between devices, body(): cotangents = (cotangent, lax.ppermute(cotangent, 'yh', SWAP))  3.19 us
  transfers between devices with their start and end apart: 28, of which 13 were waited for; matrix products, arithmetic and copies ran while one was open for 1% of the time, Pallas kernels for 26%

profile of v3, /device:TPU:2, one launch (start us, length us, event | category | flops | bytes accessed | tf_op | source)
XLA Modules:
  0.0 114.9 jit_solution(1267733702655774264)
XLA Ops:
  0.6 2.0 %collective-permute-start.3 = (bf16[512,512]{1,0:T(8,128)(2,1)}, bf16[512,512]{1,0:T(8,128)(2,1)S(1)}, u32[]{:S(2)}, u32[]{:S(2)}) collective-permute-start(bf16[512,512]{1,0:T(8,128)(2,1)} %bitcast.58), channel_id=1, source_target_pairs={{0,2},{2,4},{4,6},{6,8},{8,10},{10,12},{12,14},{14,0},{16,30},{18,... | collective-permute-start | bytes 1572872 | tf_op jit(solution)/shard_map/ppermute | solution.py:22
  2.6 3.2 %collective-permute-start = (bf16[256,512]{1,0:T(8,128)(2,1)}, bf16[256,512]{1,0:T(8,128)(2,1)S(1)}, u32[]{:S(2)}, u32[]{:S(2)}) collective-permute-start(bf16[256,512]{1,0:T(8,128)(2,1)} %refs_2_.21), channel_id=1, source_target_pairs={{0,1},{1,0},{2,3},{3,2},{4,5},{5,4},{6,7},{7,6},{8,9},{9,8},{10,11... | collective-permute-start | bytes 786440 | tf_op jit(solution)/shard_map/ppermute | solution.py:272
  5.8 2.2 %copy-done = bf16[256,8192]{1,0:T(8,128)(2,1)S(1)} copy-done((bf16[256,8192]{1,0:T(8,128)(2,1)S(1)}, bf16[256,8192]{1,0:T(8,128)(2,1)}, u32[]{:S(2)}) %copy-start) | copy-done | bytes 4194328
  10.5 3.0 %collective-permute-start.9 = (bf16[4,2,32,1024]{3,2,1,0:T(8,128)(2,1)S(1)}, bf16[4,2,32,1024]{3,2,1,0:T(8,128)(2,1)S(1)}, u32[]{:S(2)}, u32[]{:S(2)}) collective-permute-start(bf16[4,2,32,1024]{3,2,1,0:T(8,128)(2,1)S(1)} %shard_map.144), channel_id=1, source_target_pairs={{0,16},{16,0},{1,17},{17,1},{2,18},{18,2},{3,19},{19,3},{4,20},{20... | collective-permute-start | bytes 1572872 | tf_op jit(solution)/shard_map/ppermute | solution.py:300
  14.0 2.2 %copy-done.1 = bf16[256,8192]{1,0:T(8,128)(2,1)S(1)} copy-done((bf16[256,8192]{1,0:T(8,128)(2,1)S(1)}, bf16[256,8192]{1,0:T(8,128)(2,1)}, u32[]{:S(2)}) %copy-start.1) | copy-done | bytes 4194328
  16.2 3.4 %shard_map.137 = (bf16[8,256,512]{2,1,0:T(8,128)(2,1)}, bf16[2,256,512]{2,1,0:T(8,128)(2,1)}, bf16[3,256,512]{2,1,0:T(8,128)(2,1)}, bf16[2,256,512]{2,1,0:T(8,128)(2,1)}) custom-call(s32[15]{0:T(128)S(1)} %stack.124.refs_0_, bf16[256,8192]{1,0:T(8,128)(2,1)S(1)} %copy-done.1, f32[1,8192]{1,0:T(1,128)S(1)} %copy-done.5, ...), custom_call_target="tpu_custom_call" | custom-call | flops 2500000000 | bytes 12000000 | tf_op jit(solution)/shard_map/pallas_call | solution.py:59
  19.5 3.2 %collective-permute-start.1 = (bf16[2,256,512]{2,1,0:T(8,128)(2,1)}, bf16[2,256,512]{2,1,0:T(8,128)(2,1)S(1)}, u32[]{:S(2)}, u32[]{:S(2)}) collective-permute-start(bf16[2,256,512]{2,1,0:T(8,128)(2,1)} %get-tuple-element.32), channel_id=1, source_target_pairs={{0,1},{1,0},{2,3},{3,2},{4,5},{5,4},{6,7},{7,6},{8,9},{9,8},{10,11... | collective-permute-start | bytes 1572872 | tf_op jit(solution)/shard_map/ppermute | solution.py:283
  26.0 2.0 %collective-permute-start.4 = (bf16[512,512]{1,0:T(8,128)(2,1)S(1)}, bf16[512,512]{1,0:T(8,128)(2,1)S(1)}, u32[]{:S(2)}, u32[]{:S(2)}) collective-permute-start(bf16[512,512]{1,0:T(8,128)(2,1)S(1)} %shard_map.138.refs_1_), channel_id=1, source_target_pairs={{0,2},{2,4},{4,6},{6,8},{8,10},{10,12},{12,14},{14,0},{16,30},{18,... | collective-permute-start | bytes 1572872 | tf_op jit(solution)/shard_map/ppermute | solution.py:22
  28.0 5.5 %collective-permute-done.5.refs_0_.refs_5_ = bf16[512,512]{1,0:T(8,128)(2,1)S(1)} collective-permute-done((bf16[512,512]{1,0:T(8,128)(2,1)S(1)}, bf16[512,512]{1,0:T(8,128)(2,1)S(1)}, u32[]{:S(2)}, u32[]{:S(2)}) %collective-permute-start.5) | collective-permute-done | bytes 524320 | tf_op jit(solution)/shard_map/ppermute | solution.py:22
  35.9 3.2 %collective-permute-done.4.refs_4_ = bf16[512,512]{1,0:T(8,128)(2,1)S(1)} collective-permute-done((bf16[512,512]{1,0:T(8,128)(2,1)S(1)}, bf16[512,512]{1,0:T(8,128)(2,1)S(1)}, u32[]{:S(2)}, u32[]{:S(2)}) %collective-permute-start.4) | collective-permute-done | bytes 524320 | tf_op jit(solution)/shard_map/ppermute | solution.py:22
  41.7 3.1 %collective-permute-done.8.refs_0_.refs_4_ = bf16[512,512]{1,0:T(8,128)(2,1)S(1)} collective-permute-done((bf16[512,512]{1,0:T(8,128)(2,1)S(1)}, bf16[512,512]{1,0:T(8,128)(2,1)S(1)}, u32[]{:S(2)}, u32[]{:S(2)}) %collective-permute-start.8) | collective-permute-done | bytes 524320 | tf_op jit(solution)/shard_map/ppermute | solution.py:22
  46.8 4.3 %collective-permute-done.7.refs_4_ = bf16[512,512]{1,0:T(8,128)(2,1)S(1)} collective-permute-done((bf16[512,512]{1,0:T(8,128)(2,1)S(1)}, bf16[512,512]{1,0:T(8,128)(2,1)S(1)}, u32[]{:S(2)}, u32[]{:S(2)}) %collective-permute-start.7) | collective-permute-done | bytes 524320 | tf_op jit(solution)/shard_map/ppermute | solution.py:22
  54.3 2.5 %collective-permute-done.12.refs_0_.refs_5_ = bf16[512,512]{1,0:T(8,128)(2,1)S(1)} collective-permute-done((bf16[512,512]{1,0:T(8,128)(2,1)S(1)}, bf16[512,512]{1,0:T(8,128)(2,1)S(1)}, u32[]{:S(2)}, u32[]{:S(2)}) %collective-permute-start.12) | collective-permute-done | bytes 524320 | tf_op jit(solution)/shard_map/ppermute | solution.py:22
  56.9 5.4 %collective-permute-done.18.refs_1_ = bf16[1,32,1024]{2,1,0:T(8,128)(2,1)S(1)} collective-permute-done((bf16[1,32,1024]{2,1,0:T(8,128)(2,1)S(1)}, bf16[1,32,1024]{2,1,0:T(8,128)(2,1)S(1)}, u32[]{:S(2)}, u32[]{:S(2)}) %collective-permute-start.18) | collective-permute-done | bytes 65568 | tf_op jit(solution)/shard_map/ppermute | solution.py:311
  69.6 1.9 %shard_map.156 = (f32[256,512]{1,0:T(8,128)S(1)}, f32[256,512]{1,0:T(8,128)S(1)}) custom-call(bf16[8,256,512]{2,1,0:T(8,128)(2,1)} %get-tuple-element.29.refs_0_.refs_3_.refs_1_, bf16[8,256,512]{2,1,0:T(8,128)(2,1)} %get-tuple-element.29.refs_0_.refs_3_.refs_1_, bf16[2,256,512]{2,1,0:T(8,128)(2,1)} %copy-done.15, bf16[3,256,512]{2,1,0:T(8,128)(2,1)} %copy-done.14, ...), custom_call_target="tpu_custom_call" | custom-call | flops 2500000000 | bytes 12000000 | tf_op jit(solution)/shard_map/pallas_call | solution.py:59
  73.6 3.0 %collective-permute-done.17.refs_4_ = bf16[512,512]{1,0:T(8,128)(2,1)S(1)} collective-permute-done((bf16[512,512]{1,0:T(8,128)(2,1)S(1)}, bf16[512,512]{1,0:T(8,128)(2,1)S(1)}, u32[]{:S(2)}, u32[]{:S(2)}) %collective-permute-start.17) | collective-permute-done | bytes 524320 | tf_op jit(solution)/shard_map/ppermute | solution.py:22
  78.3 3.9 %collective-permute-done.16.refs_0_.refs_5_ = bf16[512,512]{1,0:T(8,128)(2,1)S(1)} collective-permute-done((bf16[512,512]{1,0:T(8,128)(2,1)S(1)}, bf16[512,512]{1,0:T(8,128)(2,1)S(1)}, u32[]{:S(2)}, u32[]{:S(2)}) %collective-permute-start.16) | collective-permute-done | bytes 524320 | tf_op jit(solution)/shard_map/ppermute | solution.py:22
  83.7 1.9 %shard_map.159 = (f32[256,512]{1,0:T(8,128)S(1)}, f32[256,512]{1,0:T(8,128)S(1)}) custom-call(bf16[8,256,512]{2,1,0:T(8,128)(2,1)} %get-tuple-element.29.refs_0_.refs_3_.refs_1_, bf16[8,256,512]{2,1,0:T(8,128)(2,1)} %get-tuple-element.29.refs_0_.refs_3_.refs_1_, bf16[3,256,512]{2,1,0:T(8,128)(2,1)} %copy-done.14, bf16[3,256,512]{2,1,0:T(8,128)(2,1)} %copy-done.14, ...), custom_call_target="tpu_custom_call" | custom-call | flops 2500000000 | bytes 12000000 | tf_op jit(solution)/shard_map/pallas_call | solution.py:59
  85.6 3.0 %collective-permute-done.22.refs_4_ = bf16[512,512]{1,0:T(8,128)(2,1)S(1)} collective-permute-done((bf16[512,512]{1,0:T(8,128)(2,1)S(1)}, bf16[512,512]{1,0:T(8,128)(2,1)S(1)}, u32[]{:S(2)}, u32[]{:S(2)}) %collective-permute-start.22) | collective-permute-done | bytes 524320 | tf_op jit(solution)/shard_map/ppermute | solution.py:22
  94.2 1.9 %shard_map.160 = (f32[256,512]{1,0:T(8,128)S(1)}, bf16[256,512]{1,0:T(8,128)(2,1)S(1)}) custom-call(bf16[8,256,512]{2,1,0:T(8,128)(2,1)} %get-tuple-element.29.refs_0_.refs_3_.refs_1_, bf16[8,256,512]{2,1,0:T(8,128)(2,1)} %get-tuple-element.29.refs_0_.refs_3_.refs_1_, bf16[2,256,512]{2,1,0:T(8,128)(2,1)} %copy-done.16, bf16[2,256,512]{2,1,0:T(8,128)(2,1)} %copy-done.16, ...), custom_call_target="tpu_custom_call" | custom-call | flops 2500000000 | bytes 12000000 | tf_op jit(solution)/shard_map/pallas_call | solution.py:59
  96.1 4.4 %collective-permute-done.24.refs_4_ = bf16[512,512]{1,0:T(8,128)(2,1)S(1)} collective-permute-done((bf16[512,512]{1,0:T(8,128)(2,1)S(1)}, bf16[512,512]{1,0:T(8,128)(2,1)S(1)}, u32[]{:S(2)}, u32[]{:S(2)}) %collective-permute-start.24) | collective-permute-done | bytes 524320 | tf_op jit(solution)/shard_map/ppermute | solution.py:22
  102.1 3.1 %collective-permute-start.21 = (bf16[256,512]{1,0:T(8,128)(2,1)S(1)}, bf16[256,512]{1,0:T(8,128)(2,1)S(1)}, u32[]{:S(2)}, u32[]{:S(2)}) collective-permute-start(bf16[256,512]{1,0:T(8,128)(2,1)S(1)} %get-tuple-element.48), channel_id=1, source_target_pairs={{0,1},{1,0},{2,3},{3,2},{4,5},{5,4},{6,7},{7,6},{8,9},{9,8},{10,11... | collective-permute-start | bytes 786440 | tf_op jit(solution)/shard_map/ppermute | solution.py:359
  106.3 3.8 %collective-permute-done.21 = bf16[256,512]{1,0:T(8,128)(2,1)S(1)} collective-permute-done((bf16[256,512]{1,0:T(8,128)(2,1)S(1)}, bf16[256,512]{1,0:T(8,128)(2,1)S(1)}, u32[]{:S(2)}, u32[]{:S(2)}) %collective-permute-start.21) | collective-permute-done | bytes 262176 | tf_op jit(solution)/shard_map/ppermute | solution.py:359
  112.5 2.4 %fusion.6 = (f32[1,512,512]{2,1,0:T(8,128)}, bf16[1,512,512]{2,1,0:T(8,128)(2,1)}, f32[1,512,512]{2,1,0:T(8,128)}) fusion(f32[512,512]{1,0:T(8,128)S(1)} %shard_map.161.refs_8_, bf16[512,512]{1,0:T(8,128)(2,1)S(1)} %collective-permute-done.26, f32[1,512,512]{2,1,0:T(8,128)S(1)} %copy-done.12, f32[1,512,512]{2,1,0:T(8,128)S(1)} %copy-done.13, ...), kind=kLoop, calls=%fused_computation.15 | loop fusion | flops 4980736 | bytes 6815744 | tf_op jit(solution)/shard_map/broadcast_in_dim | solution.py:369
  (105 shorter events, 39.4 us)
Async XLA Ops:
  0.6 22.1 %collective-permute-start.3 = (bf16[512,512]{1,0:T(8,128)(2,1)}, bf16[512,512]{1,0:T(8,128)(2,1)S(1)}, u32[]{:S(2)}, u32[]{:S(2)}) collective-permute-start(bf16[512,512]{1,0:T(8,128)(2,1)} %bitcast.58), channel_id=1, source_target_pairs={{0,2},{2,4},{4,6},{6,8},{8,10},{10,12},{12,14},{14,0},{16,30},{18,... | collective-permute-start | bytes 1572872 | tf_op jit(solution)/shard_map/ppermute | solution.py:22
  2.6 11.3 %collective-permute-start = (bf16[256,512]{1,0:T(8,128)(2,1)}, bf16[256,512]{1,0:T(8,128)(2,1)S(1)}, u32[]{:S(2)}, u32[]{:S(2)}) collective-permute-start(bf16[256,512]{1,0:T(8,128)(2,1)} %refs_2_.21), channel_id=1, source_target_pairs={{0,1},{1,0},{2,3},{3,2},{4,5},{5,4},{6,7},{7,6},{8,9},{9,8},{10,11... | collective-permute-start | bytes 786440 | tf_op jit(solution)/shard_map/ppermute | solution.py:272
  10.0 14.4 %collective-permute-start.2 = (bf16[1,256,512]{2,1,0:T(8,128)(2,1)S(1)}, bf16[1,256,512]{2,1,0:T(8,128)(2,1)}, u32[]{:S(2)}, u32[]{:S(2)}) collective-permute-start(bf16[1,256,512]{2,1,0:T(8,128)(2,1)S(1)} %get-tuple-element.33.refs_1_.refs_2_), channel_id=1, source_target_pairs={{0,1},{1,0},{2,3},{3,2},{4,5},{5,4},{6,7},{7,6},{8,9},{9,8},{10,11... | collective-permute-start | bytes 786440 | tf_op jit(solution)/shard_map/ppermute | solution.py:283
  10.5 12.6 %collective-permute-start.9 = (bf16[4,2,32,1024]{3,2,1,0:T(8,128)(2,1)S(1)}, bf16[4,2,32,1024]{3,2,1,0:T(8,128)(2,1)S(1)}, u32[]{:S(2)}, u32[]{:S(2)}) collective-permute-start(bf16[4,2,32,1024]{3,2,1,0:T(8,128)(2,1)S(1)} %shard_map.144), channel_id=1, source_target_pairs={{0,16},{16,0},{1,17},{17,1},{2,18},{18,2},{3,19},{19,3},{4,20},{20... | collective-permute-start | bytes 1572872 | tf_op jit(solution)/shard_map/ppermute | solution.py:300
  19.5 16.4 %collective-permute-start.1 = (bf16[2,256,512]{2,1,0:T(8,128)(2,1)}, bf16[2,256,512]{2,1,0:T(8,128)(2,1)S(1)}, u32[]{:S(2)}, u32[]{:S(2)}) collective-permute-start(bf16[2,256,512]{2,1,0:T(8,128)(2,1)} %get-tuple-element.32), channel_id=1, source_target_pairs={{0,1},{1,0},{2,3},{3,2},{4,5},{5,4},{6,7},{7,6},{8,9},{9,8},{10,11... | collective-permute-start | bytes 1572872 | tf_op jit(solution)/shard_map/ppermute | solution.py:283
  22.8 10.8 %collective-permute-start.5 = (bf16[512,512]{1,0:T(8,128)(2,1)S(1)}, bf16[512,512]{1,0:T(8,128)(2,1)S(1)}, u32[]{:S(2)}, u32[]{:S(2)}) collective-permute-start(bf16[512,512]{1,0:T(8,128)(2,1)S(1)} %shard_map.139), channel_id=1, source_target_pairs={{0,2},{2,4},{4,6},{6,8},{8,10},{10,12},{12,14},{14,0},{16,30},{18,... | collective-permute-start | bytes 1572872 | tf_op jit(solution)/shard_map/ppermute | solution.py:22
  23.9 9.8 %collective-permute-start.10 = (bf16[2,2,32,1024]{3,2,1,0:T(8,128)(2,1)S(1)}, bf16[2,2,32,1024]{3,2,1,0:T(8,128)(2,1)S(1)}, u32[]{:S(2)}, u32[]{:S(2)}) collective-permute-start(bf16[2,2,32,1024]{3,2,1,0:T(8,128)(2,1)S(1)} %get-tuple-element.35), channel_id=1, source_target_pairs={{0,32},{32,0},{64,96},{96,64},{1,33},{33,1},{65,97},{97,65},{2,34}... | collective-permute-start | bytes 786440 | tf_op jit(solution)/shard_map/ppermute | solution.py:305
  26.0 13.2 %collective-permute-start.4 = (bf16[512,512]{1,0:T(8,128)(2,1)S(1)}, bf16[512,512]{1,0:T(8,128)(2,1)S(1)}, u32[]{:S(2)}, u32[]{:S(2)}) collective-permute-start(bf16[512,512]{1,0:T(8,128)(2,1)S(1)} %shard_map.138.refs_1_), channel_id=1, source_target_pairs={{0,2},{2,4},{4,6},{6,8},{8,10},{10,12},{12,14},{14,0},{16,30},{18,... | collective-permute-start | bytes 1572872 | tf_op jit(solution)/shard_map/ppermute | solution.py:22
  33.6 11.2 %collective-permute-start.8 = (bf16[512,512]{1,0:T(8,128)(2,1)S(1)}, bf16[512,512]{1,0:T(8,128)(2,1)S(1)}, u32[]{:S(2)}, u32[]{:S(2)}) collective-permute-start(bf16[512,512]{1,0:T(8,128)(2,1)S(1)} %shard_map.140.refs_5_.refs_3_), channel_id=1, source_target_pairs={{0,2},{2,4},{4,6},{6,8},{8,10},{10,12},{12,14},{14,0},{16,30},{18,... | collective-permute-start | bytes 1572872 | tf_op jit(solution)/shard_map/ppermute | solution.py:22
  34.3 18.4 %collective-permute-start.13 = (bf16[1,2,32,1024]{3,2,1,0:T(8,128)(2,1)S(1)}, bf16[1,2,32,1024]{3,2,1,0:T(8,128)(2,1)S(1)}, u32[]{:S(2)}, u32[]{:S(2)}) collective-permute-start(bf16[1,2,32,1024]{3,2,1,0:T(8,128)(2,1)S(1)} %get-tuple-element.36.refs_6_), channel_id=1, source_target_pairs={{0,96},{96,0},{32,64},{64,32},{1,97},{97,1},{33,65},{65,33},{2,98}... | collective-permute-start | bytes 393224 | tf_op jit(solution)/shard_map/ppermute | solution.py:308
  40.7 10.5 %collective-permute-start.7 = (bf16[512,512]{1,0:T(8,128)(2,1)S(1)}, bf16[512,512]{1,0:T(8,128)(2,1)S(1)}, u32[]{:S(2)}, u32[]{:S(2)}) collective-permute-start(bf16[512,512]{1,0:T(8,128)(2,1)S(1)} %shard_map.141.refs_1_), channel_id=1, source_target_pairs={{0,2},{2,4},{4,6},{6,8},{8,10},{10,12},{12,14},{14,0},{16,30},{18,... | collective-permute-start | bytes 1572872 | tf_op jit(solution)/shard_map/ppermute | solution.py:22
  40.8 22.9 %collective-permute-start.6 = (bf16[3,256,512]{2,1,0:T(8,128)(2,1)S(1)}, bf16[3,256,512]{2,1,0:T(8,128)(2,1)S(1)}, u32[]{:S(2)}, u32[]{:S(2)}) collective-permute-start(bf16[3,256,512]{2,1,0:T(8,128)(2,1)S(1)} %shard_map.142.refs_7_), channel_id=1, source_target_pairs={{0,1},{1,0},{2,3},{3,2},{4,5},{5,4},{6,7},{7,6},{8,9},{9,8},{10,11... | collective-permute-start | bytes 2359304 | tf_op jit(solution)/shard_map/ppermute | solution.py:283
  44.8 11.9 %collective-permute-start.12 = (bf16[512,512]{1,0:T(8,128)(2,1)S(1)}, bf16[512,512]{1,0:T(8,128)(2,1)S(1)}, u32[]{:S(2)}, u32[]{:S(2)}) collective-permute-start(bf16[512,512]{1,0:T(8,128)(2,1)S(1)} %shard_map.143.refs_5_.refs_3_), channel_id=1, source_target_pairs={{0,2},{2,4},{4,6},{6,8},{8,10},{10,12},{12,14},{14,0},{16,30},{18,... | collective-permute-start | bytes 1572872 | tf_op jit(solution)/shard_map/ppermute | solution.py:22
  52.6 11.1 %collective-permute-start.11 = (bf16[512,512]{1,0:T(8,128)(2,1)S(1)}, bf16[512,512]{1,0:T(8,128)(2,1)S(1)}, u32[]{:S(2)}, u32[]{:S(2)}) collective-permute-start(bf16[512,512]{1,0:T(8,128)(2,1)S(1)} %shard_map.147.refs_1_), channel_id=1, source_target_pairs={{0,2},{2,4},{4,6},{6,8},{8,10},{10,12},{12,14},{14,0},{16,30},{18,... | collective-permute-start | bytes 1572872 | tf_op jit(solution)/shard_map/ppermute | solution.py:22
  56.8 12.6 %collective-permute-start.15 = (bf16[512,512]{1,0:T(8,128)(2,1)S(1)}, bf16[512,512]{1,0:T(8,128)(2,1)S(1)}, u32[]{:S(2)}, u32[]{:S(2)}) collective-permute-start(bf16[512,512]{1,0:T(8,128)(2,1)S(1)} %shard_map.148.refs_5_.refs_4_), channel_id=1, source_target_pairs={{0,2},{2,4},{4,6},{6,8},{8,10},{10,12},{12,14},{14,0},{16,30},{18,... | collective-permute-start | bytes 1572872 | tf_op jit(solution)/shard_map/ppermute | solution.py:22
  66.1 10.5 %collective-permute-start.17 = (bf16[512,512]{1,0:T(8,128)(2,1)S(1)}, bf16[512,512]{1,0:T(8,128)(2,1)S(1)}, u32[]{:S(2)}, u32[]{:S(2)}) collective-permute-start(bf16[512,512]{1,0:T(8,128)(2,1)S(1)} %shard_map.151.refs_1_), channel_id=1, source_target_pairs={{0,2},{2,4},{4,6},{6,8},{8,10},{10,12},{12,14},{14,0},{16,30},{18,... | collective-permute-start | bytes 1572872 | tf_op jit(solution)/shard_map/ppermute | solution.py:22
  67.6 23.3 %collective-permute-start.14 = (bf16[2,256,512]{2,1,0:T(8,128)(2,1)S(1)}, bf16[2,256,512]{2,1,0:T(8,128)(2,1)S(1)}, u32[]{:S(2)}, u32[]{:S(2)}) collective-permute-start(bf16[2,256,512]{2,1,0:T(8,128)(2,1)S(1)} %shard_map.152.refs_8_), channel_id=1, source_target_pairs={{0,1},{1,0},{2,3},{3,2},{4,5},{5,4},{6,7},{7,6},{8,9},{9,8},{10,11... | collective-permute-start | bytes 1572872 | tf_op jit(solution)/shard_map/ppermute | solution.py:283
  69.4 12.8 %collective-permute-start.16 = (bf16[512,512]{1,0:T(8,128)(2,1)S(1)}, bf16[512,512]{1,0:T(8,128)(2,1)S(1)}, u32[]{:S(2)}, u32[]{:S(2)}) collective-permute-start(bf16[512,512]{1,0:T(8,128)(2,1)S(1)} %shard_map.153.refs_3_.refs_5_), channel_id=1, source_target_pairs={{0,2},{2,4},{4,6},{6,8},{8,10},{10,12},{12,14},{14,0},{16,30},{18,... | collective-permute-start | bytes 1572872 | tf_op jit(solution)/shard_map/ppermute | solution.py:22
  72.1 10.4 %collective-permute-start.23 = (bf16[2,32,1024]{2,1,0:T(8,128)(2,1)S(1)}, bf16[2,32,1024]{2,1,0:T(8,128)(2,1)S(1)}, u32[]{:S(2)}, u32[]{:S(2)}) collective-permute-start(bf16[2,32,1024]{2,1,0:T(8,128)(2,1)S(1)} %shard_map.155.refs_7_), channel_id=1, source_target_pairs={{0,96},{96,0},{32,64},{64,32},{1,97},{97,1},{33,65},{65,33},{2,98}... | collective-permute-start | bytes 393224 | tf_op jit(solution)/shard_map/ppermute | solution.py:317
  78.1 10.5 %collective-permute-start.22 = (bf16[512,512]{1,0:T(8,128)(2,1)S(1)}, bf16[512,512]{1,0:T(8,128)(2,1)S(1)}, u32[]{:S(2)}, u32[]{:S(2)}) collective-permute-start(bf16[512,512]{1,0:T(8,128)(2,1)S(1)} %shard_map.157.refs_1_), channel_id=1, source_target_pairs={{0,2},{2,4},{4,6},{6,8},{8,10},{10,12},{12,14},{14,0},{16,30},{18,... | collective-permute-start | bytes 1572872 | tf_op jit(solution)/shard_map/ppermute | solution.py:22
  82.3 11.9 %collective-permute-start.20 = (bf16[512,512]{1,0:T(8,128)(2,1)S(1)}, bf16[512,512]{1,0:T(8,128)(2,1)S(1)}, u32[]{:S(2)}, u32[]{:S(2)}) collective-permute-start(bf16[512,512]{1,0:T(8,128)(2,1)S(1)} %shard_map.158.refs_3_.refs_5_), channel_id=1, source_target_pairs={{0,2},{2,4},{4,6},{6,8},{8,10},{10,12},{12,14},{14,0},{16,30},{18,... | collective-permute-start | bytes 1572872 | tf_op jit(solution)/shard_map/ppermute | solution.py:22
  90.1 10.5 %collective-permute-start.24 = (bf16[512,512]{1,0:T(8,128)(2,1)S(1)}, bf16[512,512]{1,0:T(8,128)(2,1)S(1)}, u32[]{:S(2)}, u32[]{:S(2)}) collective-permute-start(bf16[512,512]{1,0:T(8,128)(2,1)S(1)} %shard_map.163.refs_3_), channel_id=1, source_target_pairs={{0,2},{2,4},{4,6},{6,8},{8,10},{10,12},{12,14},{14,0},{16,30},{18,... | collective-permute-start | bytes 1572872 | tf_op jit(solution)/shard_map/ppermute | solution.py:22
  90.8 14.5 %collective-permute-start.27 = (bf16[4,2,32,1024]{3,2,1,0:T(8,128)(2,1)S(1)}, bf16[4,2,32,1024]{3,2,1,0:T(8,128)(2,1)S(1)}, u32[]{:S(2)}, u32[]{:S(2)}) collective-permute-start(bf16[4,2,32,1024]{3,2,1,0:T(8,128)(2,1)S(1)} %shard_map.164.refs_6_.refs_1_), channel_id=1, source_target_pairs={{0,16},{16,0},{1,17},{17,1},{2,18},{18,2},{3,19},{19,3},{4,20},{20... | collective-permute-start | bytes 1572872 | tf_op jit(solution)/shard_map/ppermute | solution.py:326
  102.0 10.5 %collective-permute-start.26 = (bf16[512,512]{1,0:T(8,128)(2,1)S(1)}, bf16[512,512]{1,0:T(8,128)(2,1)S(1)}, u32[]{:S(2)}, u32[]{:S(2)}) collective-permute-start(bf16[512,512]{1,0:T(8,128)(2,1)S(1)} %shard_map.165), channel_id=1, source_target_pairs={{0,2},{2,4},{4,6},{6,8},{8,10},{10,12},{12,14},{14,0},{16,30},{18,... | collective-permute-start | bytes 1572872 | tf_op jit(solution)/shard_map/ppermute | solution.py:22
  (21 other events, 114.1 us)
